TPU v7x, 32 devices: a whole 2x2x4 slice. The times are simulated.
32 devices in a mesh: row: 2 (over x), col: 16 (over z, y, core).
Axes of the slice: x: 2, y: 2, z: 4, core: 2. Of those that a mesh axis runs over, the one named last changes fastest.
Arguments:
- left_features: bfloat16 [8, 1024, 320], P('row', 'col'), may hold values from -6 to 6
- right_features: bfloat16 [8, 1024, 320], P('row', 'col'), may hold values from -6 to 6
- conv_weight: bfloat16 [3, 3, 3, 40, 32], replicated, may hold values from -0.1875 to 0.1875
- cotangent: bfloat16 [24, 8, 1024, 32], P(None, 'row', 'col'), may hold values from -6 to 6
Outputs:
- cost_output: bfloat16 [24, 8, 1024, 32], P(None, 'row', 'col')
- weight_grad: float32 [3, 3, 3, 40, 32], replicated
- left_grad: bfloat16 [8, 1024, 320], P('row', 'col')
- right_grad: bfloat16 [8, 1024, 320], P('row', 'col')
All inputs are finite; a program needn't handle non-finite values.
Results may differ from a plain program's by a relative error of at most 0.0049.
Values may be sent and summed in bfloat16 or wider, within the bound.
No kernel may reach another device: no remote copies, remote signals or barrier semaphores. Data moves between devices by JAX's collectives and lax.ppermute only.
A program may use at most 128 MiB of HBM per device.

v0:
```python
import functools
import math

import jax
import jax.numpy as jnp
from jax import lax
from jax.experimental import pallas as pl
from jax.experimental.pallas import tpu as pltpu
from jax.sharding import PartitionSpec as P

DISP = 24
STEP = 4
SLOT = 64
PAD = 8
F32 = jnp.float32
BF16 = jnp.bfloat16
VMEM = pl.BlockSpec(memory_space=pltpu.VMEM)
LIMIT = 16 * 1024 * 1024
BIG = 60 * 1024 * 1024


def lanes(shape):
    return lax.broadcasted_iota(jnp.int32, shape, len(shape) - 1)


def channel_table(channels, group_size, flip, value=1.0):
    shape = (group_size * SLOT, channels) if flip else (channels, group_size * SLOT)
    c = lax.broadcasted_iota(jnp.int32, shape, 1 if flip else 0)
    j = lax.broadcasted_iota(jnp.int32, shape, 0 if flip else 1)
    hit = c == (j & (SLOT - 1)) * group_size + (j >> (SLOT.bit_length() - 1))
    return jnp.where(hit, value, 0.0).astype(BF16)


def parity():
    return lax.rem(lax.axis_index("col"), 2)


def dot(a, b):
    return jnp.dot(a, b, preferred_element_type=F32)


def dot_nt(a, b):
    return lax.dot_general(a, b, (((1,), (1,)), ((), ())), preferred_element_type=F32)


def pack_kernel(left, right, ct, even, odd, r2, ctf):
    disp, rows, feat, cols = ct.shape
    base = rows * cols
    r2[...] = right[:, cols // 2 :]
    for h in range(rows):
        even[h * cols : (h + 1) * cols] = right[h]
        odd[h * cols : (h + 1) * cols] = right[h]
    for d in range(disp):
        ctf[d * cols : (d + 1) * cols] = ct[d].reshape(rows * feat, cols).astype(F32).T
    ends = []
    for col in (cols - 1, 0):
        block = ctf[pl.ds(col, disp, stride=cols), :]
        block = jnp.concatenate([block, jnp.zeros((disp, left.shape[2] - rows * feat), F32)], axis=1)
        edge = [left[h, col : col + 1].astype(F32) for h in range(rows)]
        edge += [right[h, col : col + 1].astype(F32) for h in range(rows)]
        ends.append(jnp.concatenate([block, *edge], axis=0))
    is_even = parity() == 0
    even[base:] = jnp.where(is_even, ends[0], ends[1]).astype(BF16)
    odd[base:] = jnp.where(is_even, ends[1], ends[0]).astype(BF16)


def layout_kernel(ends, left_in, right_in, ct, left, right, ctl, *rims):
    disp, rows, feat, cols = ct.shape
    per = 128 // feat
    left[...] = left_in[...]
    right[...] = right_in[...]
    for d in range(disp):
        ctl[d] = ct[d].reshape(rows * feat, cols).astype(F32).T.astype(BF16)
    for end, rim in zip(ends, rims):
        h = end()
        for q in range(disp // per):
            rim[q, PAD : PAD + cols] = jnp.concatenate(
                [ct[q * per + i, h].astype(F32) for i in range(per)], axis=0
            ).T


def end_columns(by_even, by_odd, base):
    x, y = by_even[base:].astype(F32), by_odd[base:].astype(F32)
    is_even = parity() == 0
    return jnp.where(is_even, y, x), jnp.where(is_even, x, y)


def row_kernel(ends, rows, by_even, by_odd, *rest):
    n = len(ends)
    rims, pays, (edges, buf) = rest[:n], rest[n : 2 * n], rest[2 * n :]
    count, total, _ = buf.shape
    disp = edges.shape[1]
    per, cols = disp // count, total - 2 * PAD
    feat = 128 // per
    lane = lanes((count, 128))
    for side, x in enumerate(end_columns(by_even, by_odd, rows * cols)):
        edges[side] = x[0:disp, 0:128]
    for end, rim, pay in zip(ends, rims, pays):
        h = end()
        buf[...] = rim[...]
        for side, at in ((0, PAD - 1), (1, PAD + cols)):
            out = jnp.zeros((count, 128), F32)
            for i in range(per):
                x = edges[side, pl.ds(i, count, stride=per)]
                first = pltpu.roll(x, feat * i, 1) if i else x
                last = pltpu.roll(x, (feat * (i - rows + 1)) % 128, 1) if i != rows - 1 else x
                x = jnp.where(h == 0, first, last)
                out = jnp.where((lane >= feat * i) & (lane < feat * (i + 1)), x, out)
            for q in range(count):
                buf[q, at : at + 1] = out[q : q + 1]
        pay[...] = buf[...].astype(BF16)


def volume_kernel(ends, group_size, left, right, by_even, by_odd, r2, vsh, fl, fr, fr4, *rest):
    pays, (vbuf, mixed, wide_buf) = rest[: len(ends)], rest[len(ends) :]
    rows, cols, channels = left.shape
    disp = vsh.shape[0] - 2
    reach = fr.shape[1] - cols - PAD
    wide = group_size * SLOT
    base, half = rows * cols, cols // 2
    is_even = parity() == 0
    mixed[0:base] = jnp.where(is_even, by_odd[0:base].astype(F32), by_even[0:base].astype(F32)).astype(
        BF16
    )
    mixed[base : 2 * base] = right[...].reshape(base, channels)
    mixed[2 * base : 3 * base] = left[...].reshape(base, channels)
    at_far, at_ends = 3 * base, 3 * base + base // 2
    mixed[at_far:at_ends] = r2[...].reshape(base // 2, channels)
    count = disp + 2 * rows
    for i, x in enumerate(end_columns(by_even, by_odd, base)):
        mixed[at_ends + i * count : at_ends + (i + 1) * count] = x.astype(BF16)
    wide_buf[...] = dot(mixed[...], channel_table(channels, group_size, False))
    scale = 1.0 / group_size
    for h in range(rows):
        fl[h, 0:PAD] = jnp.zeros((PAD, wide), F32)
        fl[h, PAD + cols :] = jnp.zeros((PAD, wide), F32)
        at = at_ends + disp + h
        fl[h, PAD - 1 : PAD] = wide_buf[at : at + 1] * scale
        fl[h, PAD : PAD + cols] = wide_buf[2 * base + h * cols : 2 * base + (h + 1) * cols] * scale
        at += count
        fl[h, PAD + cols : PAD + cols + 1] = wide_buf[at : at + 1] * scale
        for ref, off in ((fr, 0), (fr4, STEP)):
            start = reach - cols - half + off
            ref[h, 0:start] = jnp.zeros((start, wide), F32)
            ref[h, start : start + half] = wide_buf[at_far + h * half : at_far + (h + 1) * half]
            for part in range(2):
                at = part * base + h * cols
                to = start + half + part * cols
                ref[h, to : to + cols] = wide_buf[at : at + cols]
            to = start + half + 2 * cols
            ref[h, to:] = jnp.zeros((ref.shape[1] - to, wide), F32)
            at = at_ends + count + disp + rows + h
            ref[h, to : to + 1] = wide_buf[at : at + 1]
    vsh[0] = jnp.zeros(vsh.shape[1:], BF16)
    vsh[disp + 1] = jnp.zeros(vsh.shape[1:], BF16)
    total = cols + 2 * PAD
    block = 16
    low = lanes((block, 128)) < SLOT
    pairs = rows // 2

    def products(i, _):
        p, b = lax.rem(i, pairs), lax.div(i, pairs)
        at = pl.multiple_of(b * block, block)
        lefts = [fl[2 * p + o, pl.ds(at, block)] for o in range(2)]
        for d in range(disp):
            band = fr4 if d % 2 else fr
            start = pl.multiple_of(at + reach - PAD - 2 * STEP * (d // 2), 8)
            sums = []
            for o in range(2):
                prod = lefts[o] * band[2 * p + o, pl.ds(start, block)]
                acc = prod[:, 0:128]
                for j in range(1, wide // 128):
                    acc = acc + prod[:, 128 * j : 128 * (j + 1)]
                sums.append(acc + pltpu.roll(acc, SLOT, 1))
            vbuf[p, d, pl.ds(at, block)] = jnp.where(low, sums[0], sums[1])
        return 0

    lax.fori_loop(0, pairs * (total // block), products, 0)
    big = lanes((total, 128)) < SLOT

    def spread_taps(dd, _):
        for odd in range(2):
            d = 2 * dd + odd
            for p in range(pairs):
                for e in range(3):
                    lane = 128 * (pairs * e + p)
                    vsh[d + 1, :, lane : lane + 128] = vbuf[
                        p, d, PAD - 1 + e : PAD - 1 + e + cols
                    ].astype(BF16)
        for end, pay in zip(ends, pays):
            h = end()
            if isinstance(h, int):
                halves = [vbuf[h // 2, 2 * dd + o] for o in range(2)]
                if h % 2 == 0:
                    halves[1] = pltpu.roll(halves[1], SLOT, 1)
                else:
                    halves[0] = pltpu.roll(halves[0], SLOT, 1)
                out = jnp.where(big, halves[0], halves[1])
            else:
                last = pairs - 1
                first = jnp.where(big, vbuf[0, 2 * dd], pltpu.roll(vbuf[0, 2 * dd + 1], SLOT, 1))
                final = jnp.where(
                    big, pltpu.roll(vbuf[last, 2 * dd], SLOT, 1), vbuf[last, 2 * dd + 1]
                )
                out = jnp.where(h == 0, first, final)
            pay[pl.ds(pl.multiple_of(dd * total, 16), total)] = out.astype(BF16)
        return 0

    lax.fori_loop(0, disp // 2, spread_taps, 0)


def weight_kernel(masks, groups, vsh, ctl, by_even, by_odd, top, bot, keep_out, give_out, ctsh, vt, buf, sums):
    disp, cols, width = ctl.shape
    rows, feat = vsh.shape[2] // 3 // SLOT, 32
    per = 128 // feat
    mtop, mbot = masks()
    ctsh[0] = jnp.zeros(ctsh.shape[1:], BF16)
    ctsh[disp + 1] = jnp.zeros(ctsh.shape[1:], BF16)
    lane = lanes(top.shape[1:])
    edges = [x[0:disp, 0:128] for x in end_columns(by_even, by_odd, rows * cols)]
    for d in range(disp):
        buf[d, PAD - 1 : PAD, 0:128] = edges[0][d : d + 1]
        buf[d, PAD + cols : PAD + cols + 1, 0:128] = edges[1][d : d + 1]

    def fill(q, _):
        t = top[q].astype(F32) * mtop
        z = bot[q].astype(F32) * mbot
        for i in range(per):
            d = q * per + i
            a = t if i == 0 else pltpu.roll(t, 128 - feat * i, 1)
            y = z if i == 1 else pltpu.roll(z, (128 + feat - feat * i) % 128, 1)
            buf[d, PAD : PAD + cols, 0:128] = ctl[d].astype(F32)
            buf[d, :, 128:256] = jnp.where(lane < feat, a, jnp.where(lane < 2 * feat, y, 0.0))
            for e in range(3):
                ctsh[d + 1, :, 256 * e : 256 * (e + 1)] = buf[
                    d, PAD - 1 + e : PAD - 1 + e + cols
                ].astype(BF16)
        return 0

    lax.fori_loop(0, disp // per, fill, 0)
    step = 256 // cols
    for q in range(disp // step):
        v = vsh[1 + q * step : 1 + (q + 1) * step, :, 256:512].reshape(256, 256)
        vt[:, 256 * q : 256 * (q + 1)] = v.T
    keep = lanes((groups, 128))
    sums[...] = jnp.zeros(sums.shape, F32)

    def taps(a, _):
        for e in range(3):
            ct_block = ctsh[pl.ds(a, disp), :, 256 * e : 256 * (e + 1)].reshape(disp * cols, 256)
            full = dot(vt[...], ct_block)
            out = None
            for h in range(rows):
                x = full[SLOT * h : SLOT * h + groups, 0:128]
                y = full[SLOT * h : SLOT * h + groups, 128:256]
                if h == 0:
                    term = jnp.where(keep < feat, y, pltpu.roll(x, feat, 1))
                else:
                    term = x if h == 1 else pltpu.roll(x, 128 - feat * (h - 1), 1)
                    if h == rows - 1:
                        term = jnp.where(keep < 2 * feat, term, pltpu.roll(y, feat, 1))
                out = term if out is None else out + term
            at = pl.multiple_of(a * 128 + groups * e, 8)
            sums[pl.ds(at, groups)] = jnp.where(keep < 3 * feat, out, 0.0)
        return 0

    lax.fori_loop(0, 3, taps, 0)
    half = sums.shape[0] // 2
    is_even = parity() == 0
    low, high = sums[0:half], sums[half:]
    keep_out[...] = jnp.where(is_even, low, high)
    give_out[...] = jnp.where(is_even, high, low)


def right_kernel(ctsh, w2, fl, gv, rg0, rg1, rg2, acce, acco, both):
    disp = ctsh.shape[0] - 2
    rows, cols, channels = rg0.shape
    wide = fl.shape[2]
    group_size = wide // SLOT
    step = 512 // cols
    low = lanes((512, 128)) < SLOT

    def conv(q, _):
        acc = None
        for a in range(3):
            block = ctsh[pl.ds(q * step + a, step)].reshape(512, ctsh.shape[2])
            part = dot(block, w2[a])
            acc = part if acc is None else acc + part
        g = acc.astype(BF16).astype(F32)
        for p in range(rows // 2):
            x = g[:, 128 * p : 128 * (p + 1)]
            r = pltpu.roll(x, SLOT, 1)
            for o in range(2):
                y = jnp.where(low, r, x) if o else jnp.where(low, x, r)
                gv[2 * p + o, pl.ds(q * step, step)] = y.reshape(step, cols, 128)
        return 0

    lax.fori_loop(0, disp // step, conv, 0)
    count = cols // 8
    back = acce.shape[1] - cols
    lead = back // 8

    def right_row(h, _):
        for odd, buf in enumerate((acce, acco)):
            for k in range(lead + count):
                accs = [jnp.zeros((8, 128), F32) for _ in range(wide // 128)]
                for t in range(disp // 2):
                    b = k + t - lead
                    if b < 0 or b >= count:
                        continue
                    g = gv[h, 2 * t + odd, 8 * b : 8 * b + 8]
                    for j in range(wide // 128):
                        accs[j] = accs[j] + g * fl[
                            h, PAD + 8 * b : PAD + 8 * b + 8, 128 * j : 128 * (j + 1)
                        ]
                for j in range(wide // 128):
                    buf[h, 8 * k : 8 * k + 8, 128 * j : 128 * (j + 1)] = accs[j]
        acco[h, 8 * (lead + count) :] = jnp.zeros((8, wide), F32)
        return 0

    lax.fori_loop(0, rows, right_row, 0)
    size = back + cols
    for h in range(rows):
        both[h * size : (h + 1) * size] = (acce[h] + acco[h, STEP : STEP + size]).astype(BF16)
    whole = dot(both[...], channel_table(channels, group_size, True)).astype(BF16)
    half = cols // 2
    for h in range(rows):
        at = h * size + back
        rg2[h] = whole[at - cols - half : at - cols]
        rg1[h] = whole[at - cols : at]
        rg0[h] = whole[at : at + cols]


def left_kernel(gv, fr, fr4, lg, accl):
    rows, cols, channels = lg.shape
    disp, wide = gv.shape[1], fr.shape[2]
    group_size = wide // SLOT
    reach = fr.shape[1] - cols - PAD
    block = 16

    def left_block(i, _):
        h = lax.div(i, cols // block)
        w = pl.multiple_of(lax.rem(i, cols // block) * block, block)
        accs = [jnp.zeros((block, 128), F32) for _ in range(wide // 128)]
        for d in range(disp):
            band = fr4 if d % 2 else fr
            at = pl.multiple_of(w + reach - 2 * STEP * (d // 2), 8)
            g = gv[h, d, pl.ds(w, block)]
            for j in range(wide // 128):
                accs[j] = accs[j] + g * band[h, pl.ds(at, block), 128 * j : 128 * (j + 1)]
        for j in range(wide // 128):
            accl[h, pl.ds(w, block), 128 * j : 128 * (j + 1)] = accs[j] * (1.0 / group_size)
        return 0

    lax.fori_loop(0, rows * (cols // block), left_block, 0)
    whole = accl[...].reshape(rows * cols, wide).astype(BF16)
    out = dot(whole, channel_table(channels, group_size, True)).astype(BF16)
    lg[...] = out.reshape(rows, cols, channels)


def combine_kernel(got, rg2, out):
    cols = out.shape[1]
    half = cols // 2
    part = jnp.where(parity() == 0, 0.0, got[...].astype(F32))
    out[:, 0:half] = part[:, 0:half].astype(BF16)
    out[:, half:] = (part[:, half:] + rg2[...].astype(F32)).astype(BF16)


def conv_kernel(masks, vsh, top, bot, wc, out, halo, buf, acc):
    disp, rows, feat, cols = out.shape
    mtop, mbot = masks()
    total = buf.shape[1]
    low = lanes((total, 128)) < SLOT

    def fill(dd, _):
        at = pl.multiple_of(dd * total, 16)
        t = top[pl.ds(at, total)].astype(F32) * mtop
        b = bot[pl.ds(at, total)].astype(F32) * mbot
        buf[2 * dd] = jnp.where(low, t, pltpu.roll(b, SLOT, 1))
        buf[2 * dd + 1] = jnp.where(low, pltpu.roll(t, SLOT, 1), b)
        for o in range(2):
            for e in range(3):
                halo[2 * dd + o, :, 128 * e : 128 * (e + 1)] = buf[
                    2 * dd + o, PAD - 1 + e : PAD - 1 + e + cols
                ].astype(BF16)
        return 0

    lax.fori_loop(0, disp // 2, fill, 0)
    acc[...] = jnp.zeros(acc.shape, F32)
    step, size, depth = 512 // cols, rows * feat, vsh.shape[2]

    def conv(q, _):
        main = vsh[pl.ds(q * step + 1, step)].reshape(512, depth)
        side = halo[pl.ds(q * step, step)].reshape(512, halo.shape[2])
        taps = dot(main, wc[0:depth]) + dot(side, wc[depth:])
        for a in range(3):
            at = pl.ds(q * step + 2 - a, step)
            acc[at] = acc[at] + taps[:, size * a : size * (a + 1)].reshape(step, cols, size)
        return 0

    lax.fori_loop(0, disp // step, conv, 0)

    def store(j, _):
        x = acc[pl.ds(2 * j + 1, 2)].reshape(2 * cols, size).T
        out[2 * j] = x[:, 0:cols].astype(BF16).reshape(rows, feat, cols)
        y = pltpu.roll(x, cols, 1)
        out[2 * j + 1] = y[:, 0:cols].astype(BF16).reshape(rows, feat, cols)
        return 0

    lax.fori_loop(0, disp // 2, store, 0)


def finish_kernel(scale, mine, other, own, near, far, weight, right):
    _, _, _, feat, groups = weight.shape
    is_even = parity() == 0
    x, y = mine[...] * scale, other[...] * scale
    total = jnp.concatenate([jnp.where(is_even, x, y), jnp.where(is_even, y, x)], axis=0)
    for a in range(3):
        for e in range(3):
            at = 128 * a + groups * e
            block = total[at : at + groups].T
            for b in range(3):
                weight[2 - a, 2 - b, 2 - e] = block[feat * b : feat * (b + 1)]
    beside = jnp.where(is_even, near[...].astype(F32), 0.0)
    right[...] = (own[...].astype(F32) + beside + far[...].astype(F32)).astype(BF16)


def sum_kernel(*refs):
    *parts, out = refs
    out[...] = tree([ref[...].astype(F32) for ref in parts]).astype(out.dtype)


def tree(terms):
    while len(terms) > 1:
        terms = [terms[i] + terms[i + 1] for i in range(0, len(terms), 2)]
    return terms[0]


def taps_kernel(taps, w2, wc, turned):
    _, _, _, feat, groups = taps.shape
    rows = wc.shape[1] // 3 // feat
    depth = 3 * rows * SLOT
    low = lanes((feat, 2 * SLOT)) < SLOT
    zero = jnp.zeros((feat, 2 * SLOT), F32)

    def wide(a, b, e):
        if not 0 <= b <= 2:
            return None
        return jnp.concatenate([taps[a, b, e].astype(F32), zero[:, groups:]], axis=1)

    def beside(x, y):
        if x is None and y is None:
            return zero
        x = zero if x is None else x
        y = zero if y is None else pltpu.roll(y, SLOT, 1)
        return jnp.where(low, x, y)

    def build(a, _):
        def at_row(h):
            return pl.multiple_of((a * rows + h) * feat, feat)

        for e in range(3):
            for h in range(rows):
                for p in range(rows // 2):
                    lane = SLOT * (rows * e + 2 * p)
                    turned[pl.ds(at_row(h), feat), lane : lane + 2 * SLOT] = beside(
                        wide(a, 2 * p - h + 1, e), wide(a, 2 * p + 1 - h + 1, e)
                    )
                lane = depth + 2 * SLOT * e
                turned[pl.ds(at_row(h), feat), lane : lane + 2 * SLOT] = beside(
                    wide(a, 0, e) if h == 0 else None, wide(a, 2, e) if h == rows - 1 else None
                )
            for slot, six in enumerate((*range(1, rows + 1), 0, rows + 1)):
                at = 256 * e + feat * slot
                for p in range(rows // 2):
                    back = [2 - (six - 2 * p - o) for o in range(2)]
                    w2[a, at : at + feat, 2 * SLOT * p : 2 * SLOT * (p + 1)] = beside(
                        wide(2 - a, back[0], 2 - e), wide(2 - a, back[1], 2 - e)
                    ).astype(BF16)
            at = 256 * e + feat * (rows + 2)
            w2[a, at : 256 * (e + 1)] = jnp.zeros((256 - feat * (rows + 2), rows * SLOT), BF16)
        return 0

    lax.fori_loop(0, 3, build, 0)
    for i in range(wc.shape[0] // 128):
        for j in range(wc.shape[1] // 128):
            x, y = slice(128 * i, 128 * (i + 1)), slice(128 * j, 128 * (j + 1))
            wc[x, y] = turned[y, x].T.astype(BF16)


TOKEN = ((8, 128), F32)


def with_token(kernel, inputs, outputs):
    def run(*refs):
        kernel(*refs[: inputs + outputs], *refs[inputs + outputs + 1 :])
        refs[inputs + outputs][...] = jnp.zeros(TOKEN[0], F32)

    return run


def call(kernel, outs, scratch, *args, after=(), token=False, limit=LIMIT):
    skip = len(after)
    if token:
        kernel = with_token(kernel, len(args), len(outs))
        outs = [*outs, TOKEN]
    return pl.pallas_call(
        lambda *refs: kernel(*refs[skip:]),
        out_shape=[jax.ShapeDtypeStruct(s, t) for s, t in outs],
        in_specs=[pl.BlockSpec(memory_space=pl.ANY)] * skip + [VMEM] * len(args),
        out_specs=[VMEM] * len(outs),
        scratch_shapes=scratch,
        compiler_params=pltpu.CompilerParams(vmem_limit_bytes=limit),
    )(*after, *args)


def col_shift(block, distance):
    n = lax.axis_size("col")
    route = [(i - distance, i) for i in range(n) if 0 <= i - distance < n]
    return lax.ppermute(block, "col", route)


def row_shift(block, distance):
    n = lax.axis_size("row")
    route = [(i - distance, i) for i in range(n) if 0 <= i - distance < n]
    return lax.ppermute(block, "row", route)


def halos(pays):
    if lax.axis_size("row") == 2:
        got = lax.ppermute(pays[0], "row", [(0, 1), (1, 0)])
        return got, got
    return row_shift(pays[0], 1), row_shift(pays[1], -1)


def stages(n_row, n_col):
    col_bits = [1 << i for i in range(1, n_col.bit_length() - 1)]
    row_bits = [n_col << i for i in range(n_row.bit_length() - 1)]
    assert n_col == 2 << len(col_bits) and n_row == 1 << len(row_bits)
    bits = col_bits[:1] + row_bits + col_bits[1:]
    out = []
    for i in range(0, len(bits), 2):
        pair = bits[i : i + 2]
        out.append(pair + [sum(pair)] if len(pair) == 2 else pair)
    return out


def on_device(left_features, right_features, conv_weight, cotangent):
    rows, cols, channels = left_features.shape
    disp, feat = cotangent.shape[0], cotangent.shape[3]
    groups = conv_weight.shape[3]
    group_size = channels // groups
    wide = group_size * SLOT
    n_row, n_col = lax.axis_size("row"), lax.axis_size("col")
    per = 128 // feat

    if n_row == 2:
        ends = [lambda: (rows - 1) * (1 - lax.axis_index("row"))]
    else:
        ends = [lambda: rows - 1, lambda: 0]
    n = len(ends)

    def masks():
        at = lax.axis_index("row")
        return (
            jnp.where(at > 0, 1.0, 0.0).astype(F32),
            jnp.where(at < n_row - 1, 1.0, 0.0).astype(F32),
        )

    total = cols + 2 * PAD
    count = disp + 2 * rows
    ct = cotangent.transpose(0, 1, 3, 2)

    def swap(block, mask):
        route = [(i, i ^ mask) for i in range(n_row * n_col)]
        return lax.ppermute(block, ("row", "col"), route)

    by_even, by_odd, r2 = call(
        pack_kernel,
        [
            ((rows * cols + count, channels), BF16),
            ((rows * cols + count, channels), BF16),
            ((rows, cols // 2, channels), BF16),
        ],
        [pltpu.VMEM((disp * cols, rows * feat), F32)],
        left_features,
        right_features,
        ct,
        limit=BIG,
    )
    by_odd = lax.ppermute(
        by_odd, "col", [(i, i + 1) for i in range(1, n_col - 1, 2)] + [(i + 1, i) for i in range(1, n_col - 1, 2)]
    )
    by_even = swap(by_even, 1)
    r2 = col_shift(r2, 2)
    left_here, right_here, ctl, *rims = call(
        functools.partial(layout_kernel, ends),
        [
            ((rows, cols, channels), BF16),
            ((rows, cols, channels), BF16),
            ((disp, cols, rows * feat), BF16),
        ]
        + [((disp // per, total, 128), F32)] * n,
        [],
        left_features,
        right_features,
        ct,
    )
    w2, wc = call(
        taps_kernel,
        [((3, 3 * 256, rows * SLOT), BF16), ((3 * (rows + 2) * SLOT, 3 * rows * feat), BF16)],
        [pltpu.VMEM((3 * rows * feat, 3 * (rows + 2) * SLOT), F32)],
        conv_weight.transpose(0, 1, 2, 4, 3),
    )
    row_pays = call(
        functools.partial(row_kernel, ends, rows),
        [((disp // per, total, 128), BF16)] * n,
        [pltpu.VMEM((2, disp, 128), F32), pltpu.VMEM((disp // per, total, 128), F32)],
        by_even,
        by_odd,
        *rims,
        after=[w2],
    )
    top, bot = halos(row_pays)

    band = 104 + cols + PAD
    spread_rows = 3 * rows * cols + rows * cols // 2 + 2 * count
    vsh, fl, fr, fr4, *volume_rows = call(
        functools.partial(volume_kernel, ends, group_size),
        [
            ((disp + 2, cols, 3 * rows * SLOT), BF16),
            ((rows, total, wide), F32),
            ((rows, band, wide), F32),
            ((rows, band, wide), F32),
        ]
        + [((disp // 2 * total, 128), BF16)] * n,
        [
            pltpu.VMEM((rows // 2, disp, total, 2 * SLOT), F32),
            pltpu.VMEM((spread_rows, channels), BF16),
            pltpu.VMEM((spread_rows, wide), F32),
        ],
        left_here,
        right_here,
        by_even,
        by_odd,
        r2,
        after=row_pays,
    )
    vtop, vbot = halos(volume_rows)

    keep, give, ctsh = call(
        functools.partial(weight_kernel, masks, groups),
        [((3 * 64, 128), F32), ((3 * 64, 128), F32), ((disp + 2, cols, 3 * 256), BF16)],
        [
            pltpu.VMEM((rows * SLOT, disp * cols), BF16),
            pltpu.VMEM((disp, total, 256), F32),
            pltpu.VMEM((3 * 128, 128), F32),
        ],
        vsh, ctl, by_even, by_odd, top, bot,
    )
    got = swap(give, 1)
    gv, rg0, rg1, rg2 = call(
        right_kernel,
        [
            ((rows, disp, cols, 128), F32),
            ((rows, cols, channels), BF16),
            ((rows, cols, channels), BF16),
            ((rows, cols // 2, channels), BF16),
        ],
        [
            pltpu.VMEM((rows, cols + cols + cols // 2, wide), F32),
            pltpu.VMEM((rows, cols + cols + cols // 2 + 8, wide), F32),
            pltpu.VMEM((rows * (cols + cols + cols // 2), wide), BF16),
        ],
        ctsh, w2, fl,
    )
    rg1 = swap(rg1, 1)
    (part,) = call(sum_kernel, [(keep.shape, BF16)], [], keep, got, after=[rg0])
    output, conv_done = call(
        functools.partial(conv_kernel, masks),
        [((disp, rows, feat, cols), BF16)],
        [
            pltpu.VMEM((disp, cols, 3 * 2 * SLOT), BF16),
            pltpu.VMEM((disp, total, 128), F32),
            pltpu.VMEM((disp + 2, cols, rows * feat), F32),
        ],
        vsh, vtop, vbot, wc,
        after=[part],
        token=True,
    )
    (rg2,) = call(
        combine_kernel, [((rows, cols, channels), BF16)], [], rg1, rg2, after=[conv_done]
    )
    rg2 = col_shift(rg2, -2)
    *middle, final = stages(n_row, n_col)
    order = [conv_done]
    for stage in middle:
        parts = [part] + [swap(part, m) for m in stage]
        (part,) = call(sum_kernel, [(part.shape, BF16)], [], *parts, after=order)
        order = []
    lg, left_done = call(
        left_kernel,
        [((rows, cols, channels), BF16)],
        [pltpu.VMEM((rows, cols, wide), F32)],
        gv, fr, fr4,
        after=[part],
        token=True,
    )
    parts = [part] + [swap(part, m) for m in final]
    (part,) = call(sum_kernel, [(part.shape, F32)], [], *parts, after=[left_done])
    cells = disp * rows * n_row * cols * n_col
    weight_grad, right_grad = call(
        functools.partial(finish_kernel, 1.0 / math.sqrt(cells)),
        [((3, 3, 3, feat, groups), F32), ((rows, cols, channels), BF16)],
        [],
        part, swap(part, 1), rg0, rg1, rg2,
    )
    return (
        output.transpose(0, 1, 3, 2),
        weight_grad.transpose(0, 1, 2, 4, 3),
        lg,
        right_grad,
    )


def solution(mesh):
    in_specs = (P("row", "col", None), P("row", "col", None), P(), P(None, "row", "col", None))
    out_specs = (P(None, "row", "col", None), P(), P("row", "col", None), P("row", "col", None))
    return jax.shard_map(
        on_device, mesh=mesh, in_specs=in_specs, out_specs=out_specs, check_vma=False
    )
```

profile of v0, /device:TPU:0, one launch (start us, length us, event | category | flops | bytes accessed | tf_op | source)
XLA Modules:
  0.0 58.9 jit_solution(10747814822009766690)
XLA Ops:
  0.6 2.4 %shard_map.76 = (bf16[288,320]{1,0:T(8,128)(2,1)}, bf16[288,320]{1,0:T(8,128)(2,1)}, bf16[4,32,320]{2,1,0:T(8,128)(2,1)}) custom-call(bf16[4,64,320]{2,1,0:T(8,128)(2,1)} %refs_0_.3, bf16[4,64,320]{2,1,0:T(8,128)(2,1)} %refs_1_.3, bf16[24,4,32,64]{3,2,1,0:T(8,128)(2,1)} %bitcast.4), custom_call_target="tpu_custom_call" | custom-call | tf_op jit(solution)/shard_map/pallas_call | solution.py:507
  3.0 0.5 collective-permute-start
  3.5 0.7 %collective-permute-start.1 = (bf16[288,320]{1,0:T(8,128)(2,1)}, bf16[288,320]{1,0:T(8,128)(2,1)S(1)}, u32[]{:S(2)}, u32[]{:S(2)}) collective-permute-start(bf16[288,320]{1,0:T(8,128)(2,1)} %get-tuple-element.33), channel_id=1, source_target_pairs={{1,2},{3,4},{5,6},{7,8},{9,10},{11,12},{13,14},{2,1},{4,3},{6,5},{... | collective-permute-start | bytes 552968 | tf_op jit(solution)/shard_map/ppermute | solution.py:591
  4.2 5.7 %collective-permute-start.2 = (bf16[4,32,320]{2,1,0:T(8,128)(2,1)}, bf16[4,32,320]{2,1,0:T(8,128)(2,1)S(1)}, u32[]{:S(2)}, u32[]{:S(2)}) collective-permute-start(bf16[4,32,320]{2,1,0:T(8,128)(2,1)} %get-tuple-element.37), channel_id=1, source_target_pairs={{0,2},{1,3},{2,4},{3,5},{4,6},{5,7},{6,8},{7,9},{8,10},{9,11},{10,... | collective-permute-start | bytes 245768 | tf_op jit(solution)/shard_map/ppermute | solution.py:520
  9.8 0.0 copy-start
  9.9 1.1 %copy-done = bf16[24,4,64,32]{2,3,1,0:T(8,128)(2,1)S(1)} copy-done((bf16[24,4,64,32]{2,3,1,0:T(8,128)(2,1)S(1)}, bf16[24,4,64,32]{2,3,1,0:T(8,128)(2,1)}, u32[]{:S(2)}) %copy-start) | copy-done | bytes 393240
  11.0 0.0 copy-start.1
  11.0 0.9 %copy-done.1 = bf16[4,64,320]{2,1,0:T(8,128)(2,1)S(1)} copy-done((bf16[4,64,320]{2,1,0:T(8,128)(2,1)S(1)}, bf16[4,64,320]{2,1,0:T(8,128)(2,1)}, u32[]{:S(2)}) %copy-start.1) | copy-done | bytes 163864
  11.9 0.0 copy-start.2
  11.9 0.9 %copy-done.2 = bf16[4,64,320]{2,1,0:T(8,128)(2,1)S(1)} copy-done((bf16[4,64,320]{2,1,0:T(8,128)(2,1)S(1)}, bf16[4,64,320]{2,1,0:T(8,128)(2,1)}, u32[]{:S(2)}) %copy-start.2) | copy-done | bytes 163864
  12.8 0.3 shard_map.77
  13.2 0.0 copy-start.3
  13.2 0.9 %copy-done.3 = bf16[3,3,3,40,32]{3,4,2,1,0:T(8,128)(2,1)S(1)} copy-done((bf16[3,3,3,40,32]{3,4,2,1,0:T(8,128)(2,1)S(1)}, bf16[3,3,3,40,32]{3,4,2,1,0:T(8,128)(2,1)}, u32[]{:S(2)}) %copy-start.3) | copy-done | bytes 69144
  14.1 0.8 %shard_map.75 = (bf16[3,768,256]{2,1,0:T(8,128)(2,1)S(1)}, bf16[1152,384]{1,0:T(8,128)(2,1)S(1)}) custom-call(bf16[3,3,3,32,40]{4,3,2,1,0:T(8,128)(2,1)S(1)} %bitcast.6), custom_call_target="tpu_custom_call" | custom-call | tf_op jit(solution)/shard_map/pallas_call | solution.py:507
  14.9 0.0 collective-permute-done.refs_1_.refs_3_.refs_2_
  14.9 0.0 collective-permute-done.1.refs_2_.refs_4_.refs_3_
  14.9 0.1 shard_map.78.refs_0_
  15.0 2.2 %collective-permute-start.3 = (bf16[6,80,128]{2,1,0:T(8,128)(2,1)S(1)}, bf16[6,80,128]{2,1,0:T(8,128)(2,1)S(1)}, u32[]{:S(2)}, u32[]{:S(2)}) collective-permute-start(bf16[6,80,128]{2,1,0:T(8,128)(2,1)S(1)} %shard_map.78.refs_0_), channel_id=1, source_target_pairs={{0,16},{16,0},{1,17},{17,1},{2,18},{18,2},{3,19},{19,3},{4,20},{20... | collective-permute-start | bytes 368648 | tf_op jit(solution)/shard_map/ppermute | solution.py:531
  17.2 0.0 collective-permute-done.2.refs_5_
  17.2 3.8 %shard_map.79 = (bf16[26,64,768]{2,1,0:T(8,128)(2,1)S(1)}, f32[4,80,512]{2,1,0:T(8,128)S(1)}, f32[4,176,512]{2,1,0:T(8,128)S(1)}, f32[4,176,512]{2,1,0:T(8,128)S(1)}, bf16[960,128]{1,0:T(8,128)(2,1)S(1)}) custom-call(bf16[6,80,128]{2,1,0:T(8,128)(2,1)S(1)} %shard_map.78.refs_0_, bf16[4,64,320]{2,1,0:T(8,128)(2,1)S(1)} %get-tuple-element.35.refs_1_, ...), custom_call_target="tpu_custom_call" | custom-call | tf_op jit(solution)/shard_map/pallas_call | solution.py:507
  21.0 0.1 collective-permute-start.5
  21.0 0.0 collective-permute-done.3.refs_4_.refs_5_
  21.1 3.8 %shard_map.80 = (f32[192,128]{1,0:T(8,128)S(1)}, f32[192,128]{1,0:T(8,128)S(1)}, bf16[26,64,768]{2,1,0:T(8,128)(2,1)S(1)}) custom-call(bf16[26,64,768]{2,1,0:T(8,128)(2,1)S(1)} %get-tuple-element.38.refs_0_.refs_1_, bf16[24,64,128]{2,1,0:T(8,128)(2,1)S(1)} %get-tuple-element.39.refs_1_, bf16[288,320]{1,0:T(8,128)(2,1)S(1)} %collective-permute-done.refs_1_.refs_3_.refs_2_, ...), custom_call_target="tpu_custom_call" | custom-call | tf_op jit(solution)/shard_map/pallas_call | solution.py:507
  24.9 3.8 %shard_map.81 = (f32[4,24,64,128]{3,2,1,0:T(8,128)S(1)}, bf16[4,64,320]{2,1,0:T(8,128)(2,1)S(1)}, bf16[4,64,320]{2,1,0:T(8,128)(2,1)S(1)}, bf16[4,32,320]{2,1,0:T(8,128)(2,1)S(1)}) custom-call(bf16[26,64,768]{2,1,0:T(8,128)(2,1)S(1)} %get-tuple-element.40.refs_0_, bf16[3,768,256]{2,1,0:T(8,128)(2,1)S(1)} %get-tuple-element.31.refs_0_.refs_1_, ...), custom_call_target="tpu_custom_call" | custom-call | tf_op jit(solution)/shard_map/pallas_call | solution.py:507
  28.8 0.7 %collective-permute-start.13 = (bf16[4,64,320]{2,1,0:T(8,128)(2,1)S(1)}, bf16[4,64,320]{2,1,0:T(8,128)(2,1)S(1)}, u32[]{:S(2)}, u32[]{:S(2)}) collective-permute-start(bf16[4,64,320]{2,1,0:T(8,128)(2,1)S(1)} %get-tuple-element.53), channel_id=1, source_target_pairs={{0,1},{1,0},{2,3},{3,2},{4,5},{5,4},{6,7},{7,6},{8,9},{9,8},{10,11... | collective-permute-start | bytes 491528 | tf_op jit(solution)/shard_map/ppermute | solution.py:576
  29.5 0.1 collective-permute-start.4
  29.6 1.2 %collective-permute-done.4.refs_2_ = f32[192,128]{1,0:T(8,128)S(1)} collective-permute-done((f32[192,128]{1,0:T(8,128)S(1)}, f32[192,128]{1,0:T(8,128)S(1)}, u32[]{:S(2)}, u32[]{:S(2)}) %collective-permute-start.4) | collective-permute-done | bytes 98336 | tf_op jit(solution)/shard_map/ppermute | solution.py:576
  30.8 3.5 %collective-permute-start.8 = (bf16[192,128]{1,0:T(8,128)(2,1)S(1)}, bf16[192,128]{1,0:T(8,128)(2,1)S(1)}, u32[]{:S(2)}, u32[]{:S(2)}) collective-permute-start(bf16[192,128]{1,0:T(8,128)(2,1)S(1)} %shard_map.82.refs_0_.refs_1_), channel_id=1, source_target_pairs={{0,18},{1,19},{2,16},{3,17},{4,22},{5,23},{6,20},{7,21},{8,26},{9,... | collective-permute-start | bytes 147464 | tf_op jit(solution)/shard_map/ppermute | solution.py:576
  34.3 0.5 collective-permute-start.7
  34.9 0.1 collective-permute-start.6
  35.0 0.0 collective-permute-done.5.refs_2_.refs_3_
  35.0 6.7 %shard_map.83 = (bf16[24,4,32,64]{3,2,1,0:T(8,128)(2,1)}, f32[8,128]{1,0:T(8,128)S(1)}) custom-call(bf16[192,128]{1,0:T(8,128)(2,1)S(1)} %shard_map.82.refs_0_.refs_1_, bf16[26,64,768]{2,1,0:T(8,128)(2,1)S(1)} %get-tuple-element.38.refs_0_.refs_1_, bf16[960,128]{1,0:T(8,128)(2,1)S(1)} %collective-permute-done.5.refs_2_.refs_3_, ...), custom_call_target="tpu_custom_call" | custom-call | tf_op jit(solution)/shard_map/pallas_call | solution.py:507
  41.7 0.0 collective-permute-done.13.refs_1_.refs_3_
  41.7 0.1 shard_map.87
  41.7 1.3 %collective-permute-start.14 = (bf16[4,64,320]{2,1,0:T(8,128)(2,1)S(1)}, bf16[4,64,320]{2,1,0:T(8,128)(2,1)S(1)}, u32[]{:S(2)}, u32[]{:S(2)}) collective-permute-start(bf16[4,64,320]{2,1,0:T(8,128)(2,1)S(1)} %shard_map.87), channel_id=1, source_target_pairs={{2,0},{3,1},{4,2},{5,3},{6,4},{7,5},{8,6},{9,7},{10,8},{11,9},{12,... | collective-permute-start | bytes 491528 | tf_op jit(solution)/shard_map/ppermute | solution.py:520
  43.0 0.0 collective-permute-done.8.refs_4_
  43.0 0.0 collective-permute-done.7.refs_3_
  43.0 0.0 collective-permute-done.6.refs_2_
  43.1 6.1 %collective-permute-start.11 = (bf16[192,128]{1,0:T(8,128)(2,1)S(1)}, bf16[192,128]{1,0:T(8,128)(2,1)S(1)}, u32[]{:S(2)}, u32[]{:S(2)}) collective-permute-start(bf16[192,128]{1,0:T(8,128)(2,1)S(1)} %shard_map.84.refs_0_.refs_1_), channel_id=1, source_target_pairs={{0,12},{1,13},{2,14},{3,15},{4,8},{5,9},{6,10},{7,11},{8,4},{9,5},... | collective-permute-start | bytes 147464 | tf_op jit(solution)/shard_map/ppermute | solution.py:576
  49.2 0.0 collective-permute-start.10
  49.2 0.6 %collective-permute-start.9 = (bf16[192,128]{1,0:T(8,128)(2,1)S(1)}, bf16[192,128]{1,0:T(8,128)(2,1)S(1)}, u32[]{:S(2)}, u32[]{:S(2)}) collective-permute-start(bf16[192,128]{1,0:T(8,128)(2,1)S(1)} %shard_map.84.refs_0_.refs_1_), channel_id=1, source_target_pairs={{0,4},{1,5},{2,6},{3,7},{4,0},{5,1},{6,2},{7,3},{8,12},{9,13},{10,... | collective-permute-start | bytes 147464 | tf_op jit(solution)/shard_map/ppermute | solution.py:576
  49.8 2.6 %shard_map.85 = (bf16[4,64,320]{2,1,0:T(8,128)(2,1)}, f32[8,128]{1,0:T(8,128)S(1)}) custom-call(bf16[192,128]{1,0:T(8,128)(2,1)S(1)} %shard_map.84.refs_0_.refs_1_, f32[4,24,64,128]{3,2,1,0:T(8,128)S(1)} %get-tuple-element.49.refs_1_, f32[4,176,512]{2,1,0:T(8,128)S(1)} %get-tuple-element.50.refs_2_, f32[4,176,512]{2,1,0:T(8,128)S(1)} %get-tuple-element.51.refs_3_), custom_call_target="tpu_custom_call" | custom-call | tf_op jit(solution)/shard_map/pallas_call | solution.py:507
  52.4 3.0 %collective-permute-done.11.refs_4_ = bf16[192,128]{1,0:T(8,128)(2,1)S(1)} collective-permute-done((bf16[192,128]{1,0:T(8,128)(2,1)S(1)}, bf16[192,128]{1,0:T(8,128)(2,1)S(1)}, u32[]{:S(2)}, u32[]{:S(2)}) %collective-permute-start.11) | collective-permute-done | bytes 49184 | tf_op jit(solution)/shard_map/ppermute | solution.py:576
  55.4 1.0 %collective-permute-done.10.refs_3_ = bf16[192,128]{1,0:T(8,128)(2,1)S(1)} collective-permute-done((bf16[192,128]{1,0:T(8,128)(2,1)S(1)}, bf16[192,128]{1,0:T(8,128)(2,1)S(1)}, u32[]{:S(2)}, u32[]{:S(2)}) %collective-permute-start.10) | collective-permute-done | bytes 49184 | tf_op jit(solution)/shard_map/ppermute | solution.py:576
  56.4 0.0 collective-permute-done.9.refs_2_
  56.4 0.1 collective-permute-start.12
  56.5 1.3 %collective-permute-done.12.refs_1_ = f32[192,128]{1,0:T(8,128)S(1)} collective-permute-done((f32[192,128]{1,0:T(8,128)S(1)}, f32[192,128]{1,0:T(8,128)S(1)}, u32[]{:S(2)}, u32[]{:S(2)}) %collective-permute-start.12) | collective-permute-done | bytes 98336 | tf_op jit(solution)/shard_map/ppermute | solution.py:576
  57.8 0.0 collective-permute-done.14.refs_4_
  57.8 1.1 %shard_map.88 = (f32[3,3,3,32,40]{4,3,2,1,0:T(8,128)}, bf16[4,64,320]{2,1,0:T(8,128)(2,1)}) custom-call(f32[192,128]{1,0:T(8,128)S(1)} %shard_map.86.refs_0_, f32[192,128]{1,0:T(8,128)S(1)} %collective-permute-done.12.refs_1_, bf16[4,64,320]{2,1,0:T(8,128)(2,1)S(1)} %get-tuple-element.42.refs_0_.refs_2_, ...), custom_call_target="tpu_custom_call" | custom-call | tf_op jit(solution)/shard_map/pallas_call | solution.py:507
  (3 shorter events, 0.1 us)
Async XLA Ops:
  3.0 11.9 %collective-permute-start = (bf16[288,320]{1,0:T(8,128)(2,1)}, bf16[288,320]{1,0:T(8,128)(2,1)S(1)}, u32[]{:S(2)}, u32[]{:S(2)}) collective-permute-start(bf16[288,320]{1,0:T(8,128)(2,1)} %get-tuple-element.32), channel_id=1, source_target_pairs={{0,1},{1,0},{2,3},{3,2},{4,5},{5,4},{6,7},{7,6},{8,9},{9,8},{10,11... | collective-permute-start | bytes 552968 | tf_op jit(solution)/shard_map/ppermute | solution.py:576
  3.5 11.4 %collective-permute-start.1 = (bf16[288,320]{1,0:T(8,128)(2,1)}, bf16[288,320]{1,0:T(8,128)(2,1)S(1)}, u32[]{:S(2)}, u32[]{:S(2)}) collective-permute-start(bf16[288,320]{1,0:T(8,128)(2,1)} %get-tuple-element.33), channel_id=1, source_target_pairs={{1,2},{3,4},{5,6},{7,8},{9,10},{11,12},{13,14},{2,1},{4,3},{6,5},{... | collective-permute-start | bytes 552968 | tf_op jit(solution)/shard_map/ppermute | solution.py:591
  4.2 13.0 %collective-permute-start.2 = (bf16[4,32,320]{2,1,0:T(8,128)(2,1)}, bf16[4,32,320]{2,1,0:T(8,128)(2,1)S(1)}, u32[]{:S(2)}, u32[]{:S(2)}) collective-permute-start(bf16[4,32,320]{2,1,0:T(8,128)(2,1)} %get-tuple-element.37), channel_id=1, source_target_pairs={{0,2},{1,3},{2,4},{3,5},{4,6},{5,7},{6,8},{7,9},{8,10},{9,11},{10,... | collective-permute-start | bytes 245768 | tf_op jit(solution)/shard_map/ppermute | solution.py:520
  9.8 1.1 %copy-start = (bf16[24,4,64,32]{2,3,1,0:T(8,128)(2,1)S(1)}, bf16[24,4,64,32]{2,3,1,0:T(8,128)(2,1)}, u32[]{:S(2)}) copy-start(bf16[24,4,64,32]{2,3,1,0:T(8,128)(2,1)} %param.7) | copy-start | bytes 1179652
  11.0 0.9 %copy-start.1 = (bf16[4,64,320]{2,1,0:T(8,128)(2,1)S(1)}, bf16[4,64,320]{2,1,0:T(8,128)(2,1)}, u32[]{:S(2)}) copy-start(bf16[4,64,320]{2,1,0:T(8,128)(2,1)} %refs_0_.3) | copy-start | bytes 491524
  11.9 0.9 %copy-start.2 = (bf16[4,64,320]{2,1,0:T(8,128)(2,1)S(1)}, bf16[4,64,320]{2,1,0:T(8,128)(2,1)}, u32[]{:S(2)}) copy-start(bf16[4,64,320]{2,1,0:T(8,128)(2,1)} %refs_1_.3) | copy-start | bytes 491524
  13.2 0.9 %copy-start.3 = (bf16[3,3,3,40,32]{3,4,2,1,0:T(8,128)(2,1)S(1)}, bf16[3,3,3,40,32]{3,4,2,1,0:T(8,128)(2,1)}, u32[]{:S(2)}) copy-start(bf16[3,3,3,40,32]{3,4,2,1,0:T(8,128)(2,1)} %param.6) | copy-start | bytes 207364
  15.0 6.0 %collective-permute-start.3 = (bf16[6,80,128]{2,1,0:T(8,128)(2,1)S(1)}, bf16[6,80,128]{2,1,0:T(8,128)(2,1)S(1)}, u32[]{:S(2)}, u32[]{:S(2)}) collective-permute-start(bf16[6,80,128]{2,1,0:T(8,128)(2,1)S(1)} %shard_map.78.refs_0_), channel_id=1, source_target_pairs={{0,16},{16,0},{1,17},{17,1},{2,18},{18,2},{3,19},{19,3},{4,20},{20... | collective-permute-start | bytes 368648 | tf_op jit(solution)/shard_map/ppermute | solution.py:531
  21.0 14.0 %collective-permute-start.5 = (bf16[960,128]{1,0:T(8,128)(2,1)S(1)}, bf16[960,128]{1,0:T(8,128)(2,1)S(1)}, u32[]{:S(2)}, u32[]{:S(2)}) collective-permute-start(bf16[960,128]{1,0:T(8,128)(2,1)S(1)} %get-tuple-element.45), channel_id=1, source_target_pairs={{0,16},{16,0},{1,17},{17,1},{2,18},{18,2},{3,19},{19,3},{4,20},{20... | collective-permute-start | bytes 737288 | tf_op jit(solution)/shard_map/ppermute | solution.py:531
  28.8 12.9 %collective-permute-start.13 = (bf16[4,64,320]{2,1,0:T(8,128)(2,1)S(1)}, bf16[4,64,320]{2,1,0:T(8,128)(2,1)S(1)}, u32[]{:S(2)}, u32[]{:S(2)}) collective-permute-start(bf16[4,64,320]{2,1,0:T(8,128)(2,1)S(1)} %get-tuple-element.53), channel_id=1, source_target_pairs={{0,1},{1,0},{2,3},{3,2},{4,5},{5,4},{6,7},{7,6},{8,9},{9,8},{10,11... | collective-permute-start | bytes 491528 | tf_op jit(solution)/shard_map/ppermute | solution.py:576
  29.5 1.3 %collective-permute-start.4 = (f32[192,128]{1,0:T(8,128)S(1)}, f32[192,128]{1,0:T(8,128)S(1)}, u32[]{:S(2)}, u32[]{:S(2)}) collective-permute-start(f32[192,128]{1,0:T(8,128)S(1)} %get-tuple-element.44), channel_id=1, source_target_pairs={{0,1},{1,0},{2,3},{3,2},{4,5},{5,4},{6,7},{7,6},{8,9},{9,8},{10,11... | collective-permute-start | bytes 294920 | tf_op jit(solution)/shard_map/ppermute | solution.py:576
  30.8 12.2 %collective-permute-start.8 = (bf16[192,128]{1,0:T(8,128)(2,1)S(1)}, bf16[192,128]{1,0:T(8,128)(2,1)S(1)}, u32[]{:S(2)}, u32[]{:S(2)}) collective-permute-start(bf16[192,128]{1,0:T(8,128)(2,1)S(1)} %shard_map.82.refs_0_.refs_1_), channel_id=1, source_target_pairs={{0,18},{1,19},{2,16},{3,17},{4,22},{5,23},{6,20},{7,21},{8,26},{9,... | collective-permute-start | bytes 147464 | tf_op jit(solution)/shard_map/ppermute | solution.py:576
  34.3 8.7 %collective-permute-start.7 = (bf16[192,128]{1,0:T(8,128)(2,1)S(1)}, bf16[192,128]{1,0:T(8,128)(2,1)S(1)}, u32[]{:S(2)}, u32[]{:S(2)}) collective-permute-start(bf16[192,128]{1,0:T(8,128)(2,1)S(1)} %shard_map.82.refs_0_.refs_1_), channel_id=1, source_target_pairs={{0,16},{1,17},{2,18},{3,19},{4,20},{5,21},{6,22},{7,23},{8,24},{9,... | collective-permute-start | bytes 147464 | tf_op jit(solution)/shard_map/ppermute | solution.py:576
  34.9 8.2 %collective-permute-start.6 = (bf16[192,128]{1,0:T(8,128)(2,1)S(1)}, bf16[192,128]{1,0:T(8,128)(2,1)S(1)}, u32[]{:S(2)}, u32[]{:S(2)}) collective-permute-start(bf16[192,128]{1,0:T(8,128)(2,1)S(1)} %shard_map.82.refs_0_.refs_1_), channel_id=1, source_target_pairs={{0,2},{1,3},{2,0},{3,1},{4,6},{5,7},{6,4},{7,5},{8,10},{9,11},{10,... | collective-permute-start | bytes 147464 | tf_op jit(solution)/shard_map/ppermute | solution.py:576
  41.7 16.1 %collective-permute-start.14 = (bf16[4,64,320]{2,1,0:T(8,128)(2,1)S(1)}, bf16[4,64,320]{2,1,0:T(8,128)(2,1)S(1)}, u32[]{:S(2)}, u32[]{:S(2)}) collective-permute-start(bf16[4,64,320]{2,1,0:T(8,128)(2,1)S(1)} %shard_map.87), channel_id=1, source_target_pairs={{2,0},{3,1},{4,2},{5,3},{6,4},{7,5},{8,6},{9,7},{10,8},{11,9},{12,... | collective-permute-start | bytes 491528 | tf_op jit(solution)/shard_map/ppermute | solution.py:520
  43.1 12.3 %collective-permute-start.11 = (bf16[192,128]{1,0:T(8,128)(2,1)S(1)}, bf16[192,128]{1,0:T(8,128)(2,1)S(1)}, u32[]{:S(2)}, u32[]{:S(2)}) collective-permute-start(bf16[192,128]{1,0:T(8,128)(2,1)S(1)} %shard_map.84.refs_0_.refs_1_), channel_id=1, source_target_pairs={{0,12},{1,13},{2,14},{3,15},{4,8},{5,9},{6,10},{7,11},{8,4},{9,5},... | collective-permute-start | bytes 147464 | tf_op jit(solution)/shard_map/ppermute | solution.py:576
  49.2 7.2 %collective-permute-start.10 = (bf16[192,128]{1,0:T(8,128)(2,1)S(1)}, bf16[192,128]{1,0:T(8,128)(2,1)S(1)}, u32[]{:S(2)}, u32[]{:S(2)}) collective-permute-start(bf16[192,128]{1,0:T(8,128)(2,1)S(1)} %shard_map.84.refs_0_.refs_1_), channel_id=1, source_target_pairs={{0,8},{1,9},{2,10},{3,11},{4,12},{5,13},{6,14},{7,15},{8,0},{9,1},... | collective-permute-start | bytes 147464 | tf_op jit(solution)/shard_map/ppermute | solution.py:576
  49.2 7.2 %collective-permute-start.9 = (bf16[192,128]{1,0:T(8,128)(2,1)S(1)}, bf16[192,128]{1,0:T(8,128)(2,1)S(1)}, u32[]{:S(2)}, u32[]{:S(2)}) collective-permute-start(bf16[192,128]{1,0:T(8,128)(2,1)S(1)} %shard_map.84.refs_0_.refs_1_), channel_id=1, source_target_pairs={{0,4},{1,5},{2,6},{3,7},{4,0},{5,1},{6,2},{7,3},{8,12},{9,13},{10,... | collective-permute-start | bytes 147464 | tf_op jit(solution)/shard_map/ppermute | solution.py:576
  56.4 1.4 %collective-permute-start.12 = (f32[192,128]{1,0:T(8,128)S(1)}, f32[192,128]{1,0:T(8,128)S(1)}, u32[]{:S(2)}, u32[]{:S(2)}) collective-permute-start(f32[192,128]{1,0:T(8,128)S(1)} %shard_map.86.refs_0_), channel_id=1, source_target_pairs={{0,1},{1,0},{2,3},{3,2},{4,5},{5,4},{6,7},{7,6},{8,9},{9,8},{10,11... | collective-permute-start | bytes 294920 | tf_op jit(solution)/shard_map/ppermute | solution.py:576
where the time goes:
time: 59.2 us; the launch traced here: 58.9 us
  Pallas kernels  25.5 us (43%)
  starting transfers between devices  22.1 us (37%)
  waiting for transfers between devices  6.52 us (11%)
  local copies, waits for them, and re-layouts  3.91 us (7%)
  between operations  0.78 us (1%)
    pallas_call x14, Pallas kernels, call(): pl.pallas_call(lambda *refs: kernel(*refs[skip:]), out_shape=[jax.ShapeDt...  25.5 us
    ppermute x10, starting transfers between devices, swap(): return lax.ppermute(block, ('row', 'col'), route)  12.2 us
    ppermute x2, starting transfers between devices, col_shift(): return lax.ppermute(block, 'col', route)  6.96 us
    ppermute x10, waiting for transfers between devices, swap(): return lax.ppermute(block, ('row', 'col'), route)  6.49 us
    unnamed x8, local copies, waits for them, and re-layouts  3.91 us
    ppermute x2, starting transfers between devices, halos(): got = lax.ppermute(pays[0], 'row', [(0, 1), (1, 0)])  2.25 us
  transfers between devices with their start and end apart: 15, of which 4 were waited for; matrix products, arithmetic and copies ran while one was open for 0% of the time, Pallas kernels for 37%

commit v1 on v0

--- a/solution.py
+++ b/solution.py
@@ -16,7 +16,6 @@
 BF16 = jnp.bfloat16
 VMEM = pl.BlockSpec(memory_space=pltpu.VMEM)
 LIMIT = 16 * 1024 * 1024
-BIG = 60 * 1024 * 1024
 
 
 def lanes(shape):
@@ -43,34 +42,28 @@
     return lax.dot_general(a, b, (((1,), (1,)), ((), ())), preferred_element_type=F32)
 
 
-def pack_kernel(left, right, ct, even, odd, r2, ctf):
+def pack_kernel(ends, left, right, ct, even, odd, r2, ctl, *rest):
+    rims, ctf = rest[:-1], rest[-1]
     disp, rows, feat, cols = ct.shape
-    base = rows * cols
+    base, per = rows * cols, 128 // feat
     r2[...] = right[:, cols // 2 :]
     for h in range(rows):
         even[h * cols : (h + 1) * cols] = right[h]
         odd[h * cols : (h + 1) * cols] = right[h]
     for d in range(disp):
-        ctf[d * cols : (d + 1) * cols] = ct[d].reshape(rows * feat, cols).astype(F32).T
-    ends = []
+        block = ct[d].reshape(rows * feat, cols).astype(F32).T
+        ctf[d * cols : (d + 1) * cols] = block
+        ctl[d] = block.astype(BF16)
+    columns = []
     for col in (cols - 1, 0):
         block = ctf[pl.ds(col, disp, stride=cols), :]
         block = jnp.concatenate([block, jnp.zeros((disp, left.shape[2] - rows * feat), F32)], axis=1)
         edge = [left[h, col : col + 1].astype(F32) for h in range(rows)]
         edge += [right[h, col : col + 1].astype(F32) for h in range(rows)]
-        ends.append(jnp.concatenate([block, *edge], axis=0))
+        columns.append(jnp.concatenate([block, *edge], axis=0))
     is_even = parity() == 0
-    even[base:] = jnp.where(is_even, ends[0], ends[1]).astype(BF16)
-    odd[base:] = jnp.where(is_even, ends[1], ends[0]).astype(BF16)
-
-
-def layout_kernel(ends, left_in, right_in, ct, left, right, ctl, *rims):
-    disp, rows, feat, cols = ct.shape
-    per = 128 // feat
-    left[...] = left_in[...]
-    right[...] = right_in[...]
-    for d in range(disp):
-        ctl[d] = ct[d].reshape(rows * feat, cols).astype(F32).T.astype(BF16)
+    even[base:] = jnp.where(is_even, columns[0], columns[1]).astype(BF16)
+    odd[base:] = jnp.where(is_even, columns[1], columns[0]).astype(BF16)
     for end, rim in zip(ends, rims):
         h = end()
         for q in range(disp // per):
@@ -111,10 +104,10 @@
         pay[...] = buf[...].astype(BF16)
 
 
-def volume_kernel(ends, group_size, left, right, by_even, by_odd, r2, vsh, fl, fr, fr4, *rest):
-    pays, (vbuf, mixed, wide_buf) = rest[: len(ends)], rest[len(ends) :]
+def volume_kernel(ends, group_size, left, right, by_even, by_odd, r2, vbuf, fl, fr, fr4, *rest):
+    pays, (mixed, wide_buf) = rest[: len(ends)], rest[len(ends) :]
     rows, cols, channels = left.shape
-    disp = vsh.shape[0] - 2
+    disp = vbuf.shape[1]
     reach = fr.shape[1] - cols - PAD
     wide = group_size * SLOT
     base, half = rows * cols, cols // 2
@@ -151,8 +144,6 @@
             ref[h, to:] = jnp.zeros((ref.shape[1] - to, wide), F32)
             at = at_ends + count + disp + rows + h
             ref[h, to : to + 1] = wide_buf[at : at + 1]
-    vsh[0] = jnp.zeros(vsh.shape[1:], BF16)
-    vsh[disp + 1] = jnp.zeros(vsh.shape[1:], BF16)
     total = cols + 2 * PAD
     block = 16
     low = lanes((block, 128)) < SLOT
@@ -178,15 +169,7 @@
     lax.fori_loop(0, pairs * (total // block), products, 0)
     big = lanes((total, 128)) < SLOT
 
-    def spread_taps(dd, _):
-        for odd in range(2):
-            d = 2 * dd + odd
-            for p in range(pairs):
-                for e in range(3):
-                    lane = 128 * (pairs * e + p)
-                    vsh[d + 1, :, lane : lane + 128] = vbuf[
-                        p, d, PAD - 1 + e : PAD - 1 + e + cols
-                    ].astype(BF16)
+    for dd in range(disp // 2):
         for end, pay in zip(ends, pays):
             h = end()
             if isinstance(h, int):
@@ -203,15 +186,12 @@
                     big, pltpu.roll(vbuf[last, 2 * dd], SLOT, 1), vbuf[last, 2 * dd + 1]
                 )
                 out = jnp.where(h == 0, first, final)
-            pay[pl.ds(pl.multiple_of(dd * total, 16), total)] = out.astype(BF16)
-        return 0
-
-    lax.fori_loop(0, disp // 2, spread_taps, 0)
-
-
-def weight_kernel(masks, groups, vsh, ctl, by_even, by_odd, top, bot, keep_out, give_out, ctsh, vt, buf, sums):
+            pay[dd * total : (dd + 1) * total] = out.astype(BF16)
+
+
+def weight_kernel(masks, groups, vbuf, ctl, by_even, by_odd, top, bot, keep_out, give_out, ctsh, vt, buf, sums):
     disp, cols, width = ctl.shape
-    rows, feat = vsh.shape[2] // 3 // SLOT, 32
+    rows, feat = 2 * vbuf.shape[0], 32
     per = 128 // feat
     mtop, mbot = masks()
     ctsh[0] = jnp.zeros(ctsh.shape[1:], BF16)
@@ -237,11 +217,12 @@
                 ].astype(BF16)
         return 0
 
-    lax.fori_loop(0, disp // per, fill, 0)
+    lax.fori_loop(0, disp // per, fill, 0, unroll=True)
     step = 256 // cols
     for q in range(disp // step):
-        v = vsh[1 + q * step : 1 + (q + 1) * step, :, 256:512].reshape(256, 256)
-        vt[:, 256 * q : 256 * (q + 1)] = v.T
+        for p in range(rows // 2):
+            v = vbuf[p, q * step : (q + 1) * step, PAD : PAD + cols].reshape(256, 128).astype(BF16)
+            vt[128 * p : 128 * (p + 1), 256 * q : 256 * (q + 1)] = v.T
     keep = lanes((groups, 128))
     sums[...] = jnp.zeros(sums.shape, F32)
 
@@ -281,11 +262,8 @@
     low = lanes((512, 128)) < SLOT
 
     def conv(q, _):
-        acc = None
-        for a in range(3):
-            block = ctsh[pl.ds(q * step + a, step)].reshape(512, ctsh.shape[2])
-            part = dot(block, w2[a])
-            acc = part if acc is None else acc + part
+        slabs = [ctsh[pl.ds(q * step + a, step)].reshape(512, ctsh.shape[2]) for a in range(3)]
+        acc = dot(jnp.concatenate(slabs, axis=1), w2[...])
         g = acc.astype(BF16).astype(F32)
         for p in range(rows // 2):
             x = g[:, 128 * p : 128 * (p + 1)]
@@ -366,48 +344,54 @@
     out[:, half:] = (part[:, half:] + rg2[...].astype(F32)).astype(BF16)
 
 
-def conv_kernel(masks, vsh, top, bot, wc, out, halo, buf, acc):
+def halo_lanes(groups):
+    first = SLOT - groups
+    assert groups - first <= first
+    return (groups, SLOT, groups), (SLOT + groups, SLOT + 2 * groups - first, SLOT + groups - first)
+
+
+def place_halo(base, row, groups, offset, lane):
+    for start, end, shift in halo_lanes(groups):
+        moved = pltpu.roll(row, (shift - offset) % 128, 1)
+        base = jnp.where((lane >= start) & (lane < end), moved, base)
+    return base
+
+
+def conv_kernel(masks, groups, vbuf, top, bot, wc, out, taps, buf):
     disp, rows, feat, cols = out.shape
-    mtop, mbot = masks()
-    total = buf.shape[1]
-    low = lanes((total, 128)) < SLOT
-
-    def fill(dd, _):
-        at = pl.multiple_of(dd * total, 16)
-        t = top[pl.ds(at, total)].astype(F32) * mtop
-        b = bot[pl.ds(at, total)].astype(F32) * mbot
-        buf[2 * dd] = jnp.where(low, t, pltpu.roll(b, SLOT, 1))
-        buf[2 * dd + 1] = jnp.where(low, pltpu.roll(t, SLOT, 1), b)
-        for o in range(2):
-            for e in range(3):
-                halo[2 * dd + o, :, 128 * e : 128 * (e + 1)] = buf[
-                    2 * dd + o, PAD - 1 + e : PAD - 1 + e + cols
-                ].astype(BF16)
+    total = buf.shape[2]
+    lane = lanes((total, 128))
+    zeros = jnp.zeros((cols, taps.shape[3]), BF16)
+    taps[0, 0] = zeros
+    taps[disp // 2, 1] = zeros
+    halos_of = [(ref, mask) for ref, mask in zip((top, bot), masks())]
+    for dd in range(disp // 2):
+        for p, (ref, mask) in enumerate(halos_of):
+            row = ref[dd * total : (dd + 1) * total].astype(F32) * mask
+            for o in range(2):
+                d = 2 * dd + o
+                buf[p, d] = place_halo(vbuf[p, d], row, groups, SLOT * o, lane)
+                for e in range(3):
+                    at = 256 * e + 128 * p
+                    taps[(d + 1) // 2, (d + 1) % 2, :, at : at + 128] = buf[
+                        p, d, PAD - 1 + e : PAD - 1 + e + cols
+                    ].astype(BF16)
+    step = 6
+
+    def conv(q, _):
+        slabs = [
+            taps[pl.ds(q * step + s // 2, step), s % 2].reshape(step * cols, taps.shape[3])
+            for s in range(4)
+        ]
+        acc = dot(jnp.concatenate(slabs, axis=1), wc[...])
+        for j in range(step):
+            both = acc[j * cols : (j + 1) * cols].T.astype(BF16)
+            for o in range(2):
+                block = both[rows * feat * o : rows * feat * (o + 1)]
+                out[2 * (q * step + j) + o] = block.reshape(rows, feat, cols)
         return 0
 
-    lax.fori_loop(0, disp // 2, fill, 0)
-    acc[...] = jnp.zeros(acc.shape, F32)
-    step, size, depth = 512 // cols, rows * feat, vsh.shape[2]
-
-    def conv(q, _):
-        main = vsh[pl.ds(q * step + 1, step)].reshape(512, depth)
-        side = halo[pl.ds(q * step, step)].reshape(512, halo.shape[2])
-        taps = dot(main, wc[0:depth]) + dot(side, wc[depth:])
-        for a in range(3):
-            at = pl.ds(q * step + 2 - a, step)
-            acc[at] = acc[at] + taps[:, size * a : size * (a + 1)].reshape(step, cols, size)
-        return 0
-
-    lax.fori_loop(0, disp // step, conv, 0)
-
-    def store(j, _):
-        x = acc[pl.ds(2 * j + 1, 2)].reshape(2 * cols, size).T
-        out[2 * j] = x[:, 0:cols].astype(BF16).reshape(rows, feat, cols)
-        y = pltpu.roll(x, cols, 1)
-        out[2 * j + 1] = y[:, 0:cols].astype(BF16).reshape(rows, feat, cols)
-        return 0
-
-    lax.fori_loop(0, disp // 2, store, 0)
+    lax.fori_loop(0, disp // 2 // step, conv, 0)
 
 
 def finish_kernel(scale, mine, other, own, near, far, weight, right):
@@ -438,8 +422,8 @@
 
 def taps_kernel(taps, w2, wc, turned):
     _, _, _, feat, groups = taps.shape
-    rows = wc.shape[1] // 3 // feat
-    depth = 3 * rows * SLOT
+    rows = wc.shape[1] // 2 // feat
+    lane_of = lanes((feat, 2 * SLOT))
     low = lanes((feat, 2 * SLOT)) < SLOT
     zero = jnp.zeros((feat, 2 * SLOT), F32)
 
@@ -459,33 +443,42 @@
         def at_row(h):
             return pl.multiple_of((a * rows + h) * feat, feat)
 
+        def at_tap(row):
+            return pl.multiple_of(a * 3 * 256 + row, feat)
+
         for e in range(3):
             for h in range(rows):
                 for p in range(rows // 2):
                     lane = SLOT * (rows * e + 2 * p)
-                    turned[pl.ds(at_row(h), feat), lane : lane + 2 * SLOT] = beside(
-                        wide(a, 2 * p - h + 1, e), wide(a, 2 * p + 1 - h + 1, e)
-                    )
-                lane = depth + 2 * SLOT * e
-                turned[pl.ds(at_row(h), feat), lane : lane + 2 * SLOT] = beside(
-                    wide(a, 0, e) if h == 0 else None, wide(a, 2, e) if h == rows - 1 else None
-                )
+                    block = beside(wide(a, 2 * p - h + 1, e), wide(a, 2 * p + 1 - h + 1, e))
+                    if h == 0 and p == 0:
+                        block = place_halo(block, wide(a, 0, e), groups, 0, lane_of)
+                    if h == rows - 1 and p == rows // 2 - 1:
+                        block = place_halo(block, wide(a, 2, e), groups, 0, lane_of)
+                    turned[pl.ds(at_row(h), feat), lane : lane + 2 * SLOT] = block
             for slot, six in enumerate((*range(1, rows + 1), 0, rows + 1)):
                 at = 256 * e + feat * slot
                 for p in range(rows // 2):
                     back = [2 - (six - 2 * p - o) for o in range(2)]
-                    w2[a, at : at + feat, 2 * SLOT * p : 2 * SLOT * (p + 1)] = beside(
+                    w2[pl.ds(at_tap(at), feat), 2 * SLOT * p : 2 * SLOT * (p + 1)] = beside(
                         wide(2 - a, back[0], 2 - e), wide(2 - a, back[1], 2 - e)
                     ).astype(BF16)
             at = 256 * e + feat * (rows + 2)
-            w2[a, at : 256 * (e + 1)] = jnp.zeros((256 - feat * (rows + 2), rows * SLOT), BF16)
+            size = 256 - feat * (rows + 2)
+            w2[pl.ds(at_tap(at), size)] = jnp.zeros((size, rows * SLOT), BF16)
         return 0
 
     lax.fori_loop(0, 3, build, 0)
-    for i in range(wc.shape[0] // 128):
-        for j in range(wc.shape[1] // 128):
-            x, y = slice(128 * i, 128 * (i + 1)), slice(128 * j, 128 * (j + 1))
-            wc[x, y] = turned[y, x].T.astype(BF16)
+    depth, size = turned.shape[1], rows * feat
+    for a in range(3):
+        for i in range(depth // 128):
+            x = turned[size * a : size * (a + 1), 128 * i : 128 * (i + 1)].T.astype(BF16)
+            for o in range(2):
+                at = depth * (a + o) + 128 * i
+                wc[at : at + 128, size * o : size * (o + 1)] = x
+    for o in range(2):
+        at = depth * 3 * (1 - o)
+        wc[at : at + depth, size * o : size * (o + 1)] = jnp.zeros((depth, size), BF16)
 
 
 TOKEN = ((8, 128), F32)
@@ -499,7 +492,7 @@
     return run
 
 
-def call(kernel, outs, scratch, *args, after=(), token=False, limit=LIMIT):
+def call(kernel, outs, scratch, *args, after=(), token=False):
     skip = len(after)
     if token:
         kernel = with_token(kernel, len(args), len(outs))
@@ -510,7 +503,7 @@
         in_specs=[pl.BlockSpec(memory_space=pl.ANY)] * skip + [VMEM] * len(args),
         out_specs=[VMEM] * len(outs),
         scratch_shapes=scratch,
-        compiler_params=pltpu.CompilerParams(vmem_limit_bytes=limit),
+        compiler_params=pltpu.CompilerParams(vmem_limit_bytes=LIMIT),
     )(*after, *args)
 
 
@@ -575,41 +568,29 @@
         route = [(i, i ^ mask) for i in range(n_row * n_col)]
         return lax.ppermute(block, ("row", "col"), route)
 
-    by_even, by_odd, r2 = call(
-        pack_kernel,
+    by_even, by_odd, r2, ctl, *rims = call(
+        functools.partial(pack_kernel, ends),
         [
             ((rows * cols + count, channels), BF16),
             ((rows * cols + count, channels), BF16),
             ((rows, cols // 2, channels), BF16),
-        ],
+            ((disp, cols, rows * feat), BF16),
+        ]
+        + [((disp // per, total, 128), F32)] * n,
         [pltpu.VMEM((disp * cols, rows * feat), F32)],
         left_features,
         right_features,
         ct,
-        limit=BIG,
     )
     by_odd = lax.ppermute(
         by_odd, "col", [(i, i + 1) for i in range(1, n_col - 1, 2)] + [(i + 1, i) for i in range(1, n_col - 1, 2)]
     )
     by_even = swap(by_even, 1)
     r2 = col_shift(r2, 2)
-    left_here, right_here, ctl, *rims = call(
-        functools.partial(layout_kernel, ends),
-        [
-            ((rows, cols, channels), BF16),
-            ((rows, cols, channels), BF16),
-            ((disp, cols, rows * feat), BF16),
-        ]
-        + [((disp // per, total, 128), F32)] * n,
-        [],
-        left_features,
-        right_features,
-        ct,
-    )
     w2, wc = call(
         taps_kernel,
-        [((3, 3 * 256, rows * SLOT), BF16), ((3 * (rows + 2) * SLOT, 3 * rows * feat), BF16)],
-        [pltpu.VMEM((3 * rows * feat, 3 * (rows + 2) * SLOT), F32)],
+        [((9 * 256, rows * SLOT), BF16), ((4 * 3 * rows * SLOT, 2 * rows * feat), BF16)],
+        [pltpu.VMEM((3 * rows * feat, 3 * rows * SLOT), F32)],
         conv_weight.transpose(0, 1, 2, 4, 3),
     )
     row_pays = call(
@@ -625,22 +606,21 @@
 
     band = 104 + cols + PAD
     spread_rows = 3 * rows * cols + rows * cols // 2 + 2 * count
-    vsh, fl, fr, fr4, *volume_rows = call(
+    vbuf, fl, fr, fr4, *volume_rows = call(
         functools.partial(volume_kernel, ends, group_size),
         [
-            ((disp + 2, cols, 3 * rows * SLOT), BF16),
+            ((rows // 2, disp, total, 2 * SLOT), F32),
             ((rows, total, wide), F32),
             ((rows, band, wide), F32),
             ((rows, band, wide), F32),
         ]
         + [((disp // 2 * total, 128), BF16)] * n,
         [
-            pltpu.VMEM((rows // 2, disp, total, 2 * SLOT), F32),
             pltpu.VMEM((spread_rows, channels), BF16),
             pltpu.VMEM((spread_rows, wide), F32),
         ],
-        left_here,
-        right_here,
+        left_features,
+        right_features,
         by_even,
         by_odd,
         r2,
@@ -656,7 +636,7 @@
             pltpu.VMEM((disp, total, 256), F32),
             pltpu.VMEM((3 * 128, 128), F32),
         ],
-        vsh, ctl, by_even, by_odd, top, bot,
+        vbuf, ctl, by_even, by_odd, top, bot,
     )
     got = swap(give, 1)
     gv, rg0, rg1, rg2 = call(
@@ -677,14 +657,13 @@
     rg1 = swap(rg1, 1)
     (part,) = call(sum_kernel, [(keep.shape, BF16)], [], keep, got, after=[rg0])
     output, conv_done = call(
-        functools.partial(conv_kernel, masks),
+        functools.partial(conv_kernel, masks, groups),
         [((disp, rows, feat, cols), BF16)],
         [
-            pltpu.VMEM((disp, cols, 3 * 2 * SLOT), BF16),
-            pltpu.VMEM((disp, total, 128), F32),
-            pltpu.VMEM((disp + 2, cols, rows * feat), F32),
+            pltpu.VMEM((disp // 2 + 1, 2, cols, 3 * rows * SLOT), BF16),
+            pltpu.VMEM((rows // 2, disp, total, 128), F32),
         ],
-        vsh, vtop, vbot, wc,
+        vbuf, vtop, vbot, wc,
         after=[part],
         token=True,
     )

time: 59.2 us -> 54.8 us (0.926)
  Pallas kernels: 25.5 us -> 19.1 us
  starting transfers between devices: 22.1 us -> 23.3 us
  waiting for transfers between devices: 6.52 us -> 7.44 us
    pallas_call x14 -> x13, Pallas kernels: 25.5 us -> 19.1 us  [call(): pl.pallas_call(lambda *refs: kernel(*refs[skip:]), out_shape=[jax.ShapeDt...]
    ppermute x2, starting transfers between devices: 2.25 us -> 3.69 us  [halos(): got = lax.ppermute(pays[0], 'row', [(0, 1), (1, 0)])]
    ppermute x2, waiting for transfers between devices: 0.01 us -> 0.76 us  [col_shift(): return lax.ppermute(block, 'col', route)]
    unnamed x8 -> x12, local copies, waits for them, and re-layouts: 3.91 us -> 3.92 us
  transfers between devices with their start and end apart: 15 -> 15, of which waited for: 4 -> 5; matrix products, arithmetic and copies ran while one was open for 0% -> 0% of each run, Pallas kernels for 37% -> 32%
where the time goes in v1:
time: 54.8 us; the launch traced here: 54.5 us
  starting transfers between devices  23.3 us (43%)
  Pallas kernels  19.1 us (35%)
  waiting for transfers between devices  7.44 us (14%)
  local copies, waits for them, and re-layouts  3.92 us (7%)
  between operations  0.79 us (1%)
    pallas_call x13, Pallas kernels, call(): pl.pallas_call(lambda *refs: kernel(*refs[skip:]), out_shape=[jax.ShapeDt...  19.1 us
    ppermute x10, starting transfers between devices, swap(): return lax.ppermute(block, ('row', 'col'), route)  11.9 us
    ppermute x2, starting transfers between devices, col_shift(): return lax.ppermute(block, 'col', route)  6.99 us
    ppermute x10, waiting for transfers between devices, swap(): return lax.ppermute(block, ('row', 'col'), route)  6.68 us
    unnamed x12, local copies, waits for them, and re-layouts  3.92 us
    ppermute x2, starting transfers between devices, halos(): got = lax.ppermute(pays[0], 'row', [(0, 1), (1, 0)])  3.69 us
  transfers between devices with their start and end apart: 15, of which 5 were waited for; matrix products, arithmetic and copies ran while one was open for 0% of the time, Pallas kernels for 32%

profile of v1, /device:TPU:0, one launch (start us, length us, event | category | flops | bytes accessed | tf_op | source)
XLA Modules:
  0.0 54.5 jit_solution(13315530992509664907)
XLA Ops:
  0.6 0.0 copy-start
  0.6 0.9 %copy-done = bf16[4,64,320]{2,1,0:T(8,128)(2,1)S(1)} copy-done((bf16[4,64,320]{2,1,0:T(8,128)(2,1)S(1)}, bf16[4,64,320]{2,1,0:T(8,128)(2,1)}, u32[]{:S(2)}) %copy-start) | copy-done | bytes 163864
  1.6 0.0 copy-start.2
  1.6 0.9 %copy-done.2 = bf16[4,64,320]{2,1,0:T(8,128)(2,1)S(1)} copy-done((bf16[4,64,320]{2,1,0:T(8,128)(2,1)S(1)}, bf16[4,64,320]{2,1,0:T(8,128)(2,1)}, u32[]{:S(2)}) %copy-start.2) | copy-done | bytes 163864
  2.5 0.0 copy-start.4
  2.5 1.1 %copy-done.4 = bf16[24,4,64,32]{2,3,1,0:T(8,128)(2,1)S(1)} copy-done((bf16[24,4,64,32]{2,3,1,0:T(8,128)(2,1)S(1)}, bf16[24,4,64,32]{2,3,1,0:T(8,128)(2,1)}, u32[]{:S(2)}) %copy-start.4) | copy-done | bytes 393240
  3.6 0.0 copy-start.1
  3.6 0.0 copy-start.3
  3.6 0.3 shard_map.76
  4.0 0.5 collective-permute-start
  4.5 0.7 %collective-permute-start.1 = (bf16[288,320]{1,0:T(8,128)(2,1)S(1)}, bf16[288,320]{1,0:T(8,128)(2,1)S(1)}, u32[]{:S(2)}, u32[]{:S(2)}) collective-permute-start(bf16[288,320]{1,0:T(8,128)(2,1)S(1)} %get-tuple-element.31), channel_id=1, source_target_pairs={{1,2},{3,4},{5,6},{7,8},{9,10},{11,12},{13,14},{2,1},{4,3},{6,5},{... | collective-permute-start | bytes 552968 | tf_op jit(solution)/shard_map/ppermute | solution.py:585
  5.2 5.7 %collective-permute-start.2 = (bf16[4,32,320]{2,1,0:T(8,128)(2,1)S(1)}, bf16[4,32,320]{2,1,0:T(8,128)(2,1)S(1)}, u32[]{:S(2)}, u32[]{:S(2)}) collective-permute-start(bf16[4,32,320]{2,1,0:T(8,128)(2,1)S(1)} %get-tuple-element.33), channel_id=1, source_target_pairs={{0,2},{1,3},{2,4},{3,5},{4,6},{5,7},{6,8},{7,9},{8,10},{9,11},{10,... | collective-permute-start | bytes 245768 | tf_op jit(solution)/shard_map/ppermute | solution.py:513
  10.9 0.0 copy-start.5
  10.9 0.9 %copy-done.5 = bf16[3,3,3,40,32]{3,4,2,1,0:T(8,128)(2,1)S(1)} copy-done((bf16[3,3,3,40,32]{3,4,2,1,0:T(8,128)(2,1)S(1)}, bf16[3,3,3,40,32]{3,4,2,1,0:T(8,128)(2,1)}, u32[]{:S(2)}) %copy-start.5) | copy-done | bytes 69144
  11.8 0.8 %shard_map.75 = (bf16[2304,256]{1,0:T(8,128)(2,1)S(1)}, bf16[3072,256]{1,0:T(8,128)(2,1)S(1)}) custom-call(bf16[3,3,3,32,40]{4,3,2,1,0:T(8,128)(2,1)S(1)} %bitcast.5), custom_call_target="tpu_custom_call" | custom-call | tf_op jit(solution)/shard_map/pallas_call | solution.py:500
  12.6 0.0 collective-permute-done.refs_1_.refs_3_.refs_2_
  12.6 0.0 collective-permute-done.1.refs_2_.refs_4_.refs_3_
  12.6 0.1 shard_map.77.refs_0_
  12.7 2.1 %collective-permute-start.3 = (bf16[6,80,128]{2,1,0:T(8,128)(2,1)S(1)}, bf16[6,80,128]{2,1,0:T(8,128)(2,1)S(1)}, u32[]{:S(2)}, u32[]{:S(2)}) collective-permute-start(bf16[6,80,128]{2,1,0:T(8,128)(2,1)S(1)} %shard_map.77.refs_0_), channel_id=1, source_target_pairs={{0,16},{16,0},{1,17},{17,1},{2,18},{18,2},{3,19},{19,3},{4,20},{20... | collective-permute-start | bytes 368648 | tf_op jit(solution)/shard_map/ppermute | solution.py:524
  14.9 0.8 %collective-permute-done.2.refs_5_ = bf16[4,32,320]{2,1,0:T(8,128)(2,1)S(1)} collective-permute-done((bf16[4,32,320]{2,1,0:T(8,128)(2,1)S(1)}, bf16[4,32,320]{2,1,0:T(8,128)(2,1)S(1)}, u32[]{:S(2)}, u32[]{:S(2)}) %collective-permute-start.2) | collective-permute-done | bytes 81952 | tf_op jit(solution)/shard_map/ppermute | solution.py:513
  15.6 0.0 copy-done.1
  15.6 0.0 copy-done.3
  15.6 2.8 %shard_map.78 = (f32[2,24,80,128]{3,2,1,0:T(8,128)S(1)}, f32[4,80,512]{2,1,0:T(8,128)S(1)}, f32[4,176,512]{2,1,0:T(8,128)S(1)}, f32[4,176,512]{2,1,0:T(8,128)S(1)}, bf16[960,128]{1,0:T(8,128)(2,1)S(1)}) custom-call(bf16[6,80,128]{2,1,0:T(8,128)(2,1)S(1)} %shard_map.77.refs_0_, bf16[4,64,320]{2,1,0:T(8,128)(2,1)S(1)} %copy-done.1, ...), custom_call_target="tpu_custom_call" | custom-call | tf_op jit(solution)/shard_map/pallas_call | solution.py:500
  18.4 1.6 %collective-permute-start.5 = (bf16[960,128]{1,0:T(8,128)(2,1)S(1)}, bf16[960,128]{1,0:T(8,128)(2,1)S(1)}, u32[]{:S(2)}, u32[]{:S(2)}) collective-permute-start(bf16[960,128]{1,0:T(8,128)(2,1)S(1)} %get-tuple-element.41), channel_id=1, source_target_pairs={{0,16},{16,0},{1,17},{17,1},{2,18},{18,2},{3,19},{19,3},{4,20},{20... | collective-permute-start | bytes 737288 | tf_op jit(solution)/shard_map/ppermute | solution.py:524
  20.0 0.0 collective-permute-done.3.refs_4_.refs_5_
  20.0 3.5 %shard_map.79 = (f32[192,128]{1,0:T(8,128)S(1)}, f32[192,128]{1,0:T(8,128)S(1)}, bf16[26,64,768]{2,1,0:T(8,128)(2,1)S(1)}) custom-call(f32[2,24,80,128]{3,2,1,0:T(8,128)S(1)} %get-tuple-element.34.refs_0_.refs_1_, bf16[24,64,128]{2,1,0:T(8,128)(2,1)S(1)} %get-tuple-element.35.refs_1_, bf16[288,320]{1,0:T(8,128)(2,1)S(1)} %collective-permute-done.refs_1_.refs_3_.refs_2_, ...), custom_call_target="tpu_custom_call" | custom-call | tf_op jit(solution)/shard_map/pallas_call | solution.py:500
  23.4 3.9 %shard_map.80 = (f32[4,24,64,128]{3,2,1,0:T(8,128)S(1)}, bf16[4,64,320]{2,1,0:T(8,128)(2,1)S(1)}, bf16[4,64,320]{2,1,0:T(8,128)(2,1)S(1)}, bf16[4,32,320]{2,1,0:T(8,128)(2,1)S(1)}) custom-call(bf16[26,64,768]{2,1,0:T(8,128)(2,1)S(1)} %get-tuple-element.36.refs_0_, bf16[2304,256]{1,0:T(8,128)(2,1)S(1)} %get-tuple-element.29.refs_0_.refs_1_, ...), custom_call_target="tpu_custom_call" | custom-call | tf_op jit(solution)/shard_map/pallas_call | solution.py:500
  27.3 0.5 %collective-permute-start.13 = (bf16[4,64,320]{2,1,0:T(8,128)(2,1)S(1)}, bf16[4,64,320]{2,1,0:T(8,128)(2,1)S(1)}, u32[]{:S(2)}, u32[]{:S(2)}) collective-permute-start(bf16[4,64,320]{2,1,0:T(8,128)(2,1)S(1)} %get-tuple-element.49), channel_id=1, source_target_pairs={{0,1},{1,0},{2,3},{3,2},{4,5},{5,4},{6,7},{7,6},{8,9},{9,8},{10,11... | collective-permute-start | bytes 491528 | tf_op jit(solution)/shard_map/ppermute | solution.py:569
  27.9 0.1 collective-permute-start.4
  28.0 1.2 %collective-permute-done.4.refs_2_ = f32[192,128]{1,0:T(8,128)S(1)} collective-permute-done((f32[192,128]{1,0:T(8,128)S(1)}, f32[192,128]{1,0:T(8,128)S(1)}, u32[]{:S(2)}, u32[]{:S(2)}) %collective-permute-start.4) | collective-permute-done | bytes 98336 | tf_op jit(solution)/shard_map/ppermute | solution.py:569
  29.2 3.2 %collective-permute-start.8 = (bf16[192,128]{1,0:T(8,128)(2,1)S(1)}, bf16[192,128]{1,0:T(8,128)(2,1)S(1)}, u32[]{:S(2)}, u32[]{:S(2)}) collective-permute-start(bf16[192,128]{1,0:T(8,128)(2,1)S(1)} %shard_map.81.refs_0_.refs_1_), channel_id=1, source_target_pairs={{0,18},{1,19},{2,16},{3,17},{4,22},{5,23},{6,20},{7,21},{8,26},{9,... | collective-permute-start | bytes 147464 | tf_op jit(solution)/shard_map/ppermute | solution.py:569
  32.4 0.6 %collective-permute-start.7 = (bf16[192,128]{1,0:T(8,128)(2,1)S(1)}, bf16[192,128]{1,0:T(8,128)(2,1)S(1)}, u32[]{:S(2)}, u32[]{:S(2)}) collective-permute-start(bf16[192,128]{1,0:T(8,128)(2,1)S(1)} %shard_map.81.refs_0_.refs_1_), channel_id=1, source_target_pairs={{0,16},{1,17},{2,18},{3,19},{4,20},{5,21},{6,22},{7,23},{8,24},{9,... | collective-permute-start | bytes 147464 | tf_op jit(solution)/shard_map/ppermute | solution.py:569
  33.0 0.0 collective-permute-start.6
  33.0 0.0 collective-permute-done.5.refs_2_.refs_3_
  33.0 3.9 %shard_map.82 = (bf16[24,4,32,64]{3,2,1,0:T(8,128)(2,1)}, f32[8,128]{1,0:T(8,128)S(1)}) custom-call(bf16[192,128]{1,0:T(8,128)(2,1)S(1)} %shard_map.81.refs_0_.refs_1_, f32[2,24,80,128]{3,2,1,0:T(8,128)S(1)} %get-tuple-element.34.refs_0_.refs_1_, bf16[960,128]{1,0:T(8,128)(2,1)S(1)} %collective-permute-done.5.refs_2_.refs_3_, ...), custom_call_target="tpu_custom_call" | custom-call | tf_op jit(solution)/shard_map/pallas_call | solution.py:500
  36.9 0.0 collective-permute-done.13.refs_1_.refs_3_
  36.9 0.1 shard_map.86
  37.0 1.3 %collective-permute-start.14 = (bf16[4,64,320]{2,1,0:T(8,128)(2,1)S(1)}, bf16[4,64,320]{2,1,0:T(8,128)(2,1)S(1)}, u32[]{:S(2)}, u32[]{:S(2)}) collective-permute-start(bf16[4,64,320]{2,1,0:T(8,128)(2,1)S(1)} %shard_map.86), channel_id=1, source_target_pairs={{2,0},{3,1},{4,2},{5,3},{6,4},{7,5},{8,6},{9,7},{10,8},{11,9},{12,... | collective-permute-start | bytes 491528 | tf_op jit(solution)/shard_map/ppermute | solution.py:513
  38.3 0.0 collective-permute-done.8.refs_4_
  38.3 0.0 collective-permute-done.7.refs_3_
  38.3 0.0 collective-permute-done.6.refs_2_
  38.4 6.2 %collective-permute-start.11 = (bf16[192,128]{1,0:T(8,128)(2,1)S(1)}, bf16[192,128]{1,0:T(8,128)(2,1)S(1)}, u32[]{:S(2)}, u32[]{:S(2)}) collective-permute-start(bf16[192,128]{1,0:T(8,128)(2,1)S(1)} %shard_map.83.refs_0_.refs_1_), channel_id=1, source_target_pairs={{0,12},{1,13},{2,14},{3,15},{4,8},{5,9},{6,10},{7,11},{8,4},{9,5},... | collective-permute-start | bytes 147464 | tf_op jit(solution)/shard_map/ppermute | solution.py:569
  44.6 0.0 collective-permute-start.10
  44.6 0.6 %collective-permute-start.9 = (bf16[192,128]{1,0:T(8,128)(2,1)S(1)}, bf16[192,128]{1,0:T(8,128)(2,1)S(1)}, u32[]{:S(2)}, u32[]{:S(2)}) collective-permute-start(bf16[192,128]{1,0:T(8,128)(2,1)S(1)} %shard_map.83.refs_0_.refs_1_), channel_id=1, source_target_pairs={{0,4},{1,5},{2,6},{3,7},{4,0},{5,1},{6,2},{7,3},{8,12},{9,13},{10,... | collective-permute-start | bytes 147464 | tf_op jit(solution)/shard_map/ppermute | solution.py:569
  45.3 2.6 %shard_map.84 = (bf16[4,64,320]{2,1,0:T(8,128)(2,1)}, f32[8,128]{1,0:T(8,128)S(1)}) custom-call(bf16[192,128]{1,0:T(8,128)(2,1)S(1)} %shard_map.83.refs_0_.refs_1_, f32[4,24,64,128]{3,2,1,0:T(8,128)S(1)} %get-tuple-element.45.refs_1_, f32[4,176,512]{2,1,0:T(8,128)S(1)} %get-tuple-element.46.refs_2_, f32[4,176,512]{2,1,0:T(8,128)S(1)} %get-tuple-element.47.refs_3_), custom_call_target="tpu_custom_call" | custom-call | tf_op jit(solution)/shard_map/pallas_call | solution.py:500
  47.9 3.2 %collective-permute-done.11.refs_4_ = bf16[192,128]{1,0:T(8,128)(2,1)S(1)} collective-permute-done((bf16[192,128]{1,0:T(8,128)(2,1)S(1)}, bf16[192,128]{1,0:T(8,128)(2,1)S(1)}, u32[]{:S(2)}, u32[]{:S(2)}) %collective-permute-start.11) | collective-permute-done | bytes 49184 | tf_op jit(solution)/shard_map/ppermute | solution.py:569
  51.0 1.0 %collective-permute-done.10.refs_3_ = bf16[192,128]{1,0:T(8,128)(2,1)S(1)} collective-permute-done((bf16[192,128]{1,0:T(8,128)(2,1)S(1)}, bf16[192,128]{1,0:T(8,128)(2,1)S(1)}, u32[]{:S(2)}, u32[]{:S(2)}) %collective-permute-start.10) | collective-permute-done | bytes 49184 | tf_op jit(solution)/shard_map/ppermute | solution.py:569
  52.0 0.0 collective-permute-done.9.refs_2_
  52.1 0.1 collective-permute-start.12
  52.1 1.3 %collective-permute-done.12.refs_1_ = f32[192,128]{1,0:T(8,128)S(1)} collective-permute-done((f32[192,128]{1,0:T(8,128)S(1)}, f32[192,128]{1,0:T(8,128)S(1)}, u32[]{:S(2)}, u32[]{:S(2)}) %collective-permute-start.12) | collective-permute-done | bytes 98336 | tf_op jit(solution)/shard_map/ppermute | solution.py:569
  53.4 0.0 collective-permute-done.14.refs_4_
  53.4 1.1 %shard_map.87 = (f32[3,3,3,32,40]{4,3,2,1,0:T(8,128)}, bf16[4,64,320]{2,1,0:T(8,128)(2,1)}) custom-call(f32[192,128]{1,0:T(8,128)S(1)} %shard_map.85.refs_0_, f32[192,128]{1,0:T(8,128)S(1)} %collective-permute-done.12.refs_1_, bf16[4,64,320]{2,1,0:T(8,128)(2,1)S(1)} %get-tuple-element.38.refs_0_.refs_2_, ...), custom_call_target="tpu_custom_call" | custom-call | tf_op jit(solution)/shard_map/pallas_call | solution.py:500
  (3 shorter events, 0.1 us)
Async XLA Ops:
  0.6 0.9 %copy-start = (bf16[4,64,320]{2,1,0:T(8,128)(2,1)S(1)}, bf16[4,64,320]{2,1,0:T(8,128)(2,1)}, u32[]{:S(2)}) copy-start(bf16[4,64,320]{2,1,0:T(8,128)(2,1)} %refs_1_.3) | copy-start | bytes 491524
  1.6 0.9 %copy-start.2 = (bf16[4,64,320]{2,1,0:T(8,128)(2,1)S(1)}, bf16[4,64,320]{2,1,0:T(8,128)(2,1)}, u32[]{:S(2)}) copy-start(bf16[4,64,320]{2,1,0:T(8,128)(2,1)} %refs_2_.1) | copy-start | bytes 491524
  2.5 1.1 %copy-start.4 = (bf16[24,4,64,32]{2,3,1,0:T(8,128)(2,1)S(1)}, bf16[24,4,64,32]{2,3,1,0:T(8,128)(2,1)}, u32[]{:S(2)}) copy-start(bf16[24,4,64,32]{2,3,1,0:T(8,128)(2,1)} %param.7) | copy-start | bytes 1179652
  3.6 12.0 %copy-start.1 = (bf16[4,64,320]{2,1,0:T(8,128)(2,1)S(1)}, bf16[4,64,320]{2,1,0:T(8,128)(2,1)}, u32[]{:S(2)}) copy-start(bf16[4,64,320]{2,1,0:T(8,128)(2,1)} %refs_1_.3) | copy-start | bytes 491524
  3.6 12.0 %copy-start.3 = (bf16[4,64,320]{2,1,0:T(8,128)(2,1)S(1)}, bf16[4,64,320]{2,1,0:T(8,128)(2,1)}, u32[]{:S(2)}) copy-start(bf16[4,64,320]{2,1,0:T(8,128)(2,1)} %refs_2_.1) | copy-start | bytes 491524
  4.0 8.6 %collective-permute-start = (bf16[288,320]{1,0:T(8,128)(2,1)S(1)}, bf16[288,320]{1,0:T(8,128)(2,1)S(1)}, u32[]{:S(2)}, u32[]{:S(2)}) collective-permute-start(bf16[288,320]{1,0:T(8,128)(2,1)S(1)} %get-tuple-element.30), channel_id=1, source_target_pairs={{0,1},{1,0},{2,3},{3,2},{4,5},{5,4},{6,7},{7,6},{8,9},{9,8},{10,11... | collective-permute-start | bytes 552968 | tf_op jit(solution)/shard_map/ppermute | solution.py:569
  4.5 8.1 %collective-permute-start.1 = (bf16[288,320]{1,0:T(8,128)(2,1)S(1)}, bf16[288,320]{1,0:T(8,128)(2,1)S(1)}, u32[]{:S(2)}, u32[]{:S(2)}) collective-permute-start(bf16[288,320]{1,0:T(8,128)(2,1)S(1)} %get-tuple-element.31), channel_id=1, source_target_pairs={{1,2},{3,4},{5,6},{7,8},{9,10},{11,12},{13,14},{2,1},{4,3},{6,5},{... | collective-permute-start | bytes 552968 | tf_op jit(solution)/shard_map/ppermute | solution.py:585
  5.2 10.5 %collective-permute-start.2 = (bf16[4,32,320]{2,1,0:T(8,128)(2,1)S(1)}, bf16[4,32,320]{2,1,0:T(8,128)(2,1)S(1)}, u32[]{:S(2)}, u32[]{:S(2)}) collective-permute-start(bf16[4,32,320]{2,1,0:T(8,128)(2,1)S(1)} %get-tuple-element.33), channel_id=1, source_target_pairs={{0,2},{1,3},{2,4},{3,5},{4,6},{5,7},{6,8},{7,9},{8,10},{9,11},{10,... | collective-permute-start | bytes 245768 | tf_op jit(solution)/shard_map/ppermute | solution.py:513
  10.9 0.9 %copy-start.5 = (bf16[3,3,3,40,32]{3,4,2,1,0:T(8,128)(2,1)S(1)}, bf16[3,3,3,40,32]{3,4,2,1,0:T(8,128)(2,1)}, u32[]{:S(2)}) copy-start(bf16[3,3,3,40,32]{3,4,2,1,0:T(8,128)(2,1)} %param.6) | copy-start | bytes 207364
  12.7 7.2 %collective-permute-start.3 = (bf16[6,80,128]{2,1,0:T(8,128)(2,1)S(1)}, bf16[6,80,128]{2,1,0:T(8,128)(2,1)S(1)}, u32[]{:S(2)}, u32[]{:S(2)}) collective-permute-start(bf16[6,80,128]{2,1,0:T(8,128)(2,1)S(1)} %shard_map.77.refs_0_), channel_id=1, source_target_pairs={{0,16},{16,0},{1,17},{17,1},{2,18},{18,2},{3,19},{19,3},{4,20},{20... | collective-permute-start | bytes 368648 | tf_op jit(solution)/shard_map/ppermute | solution.py:524
  18.4 14.6 %collective-permute-start.5 = (bf16[960,128]{1,0:T(8,128)(2,1)S(1)}, bf16[960,128]{1,0:T(8,128)(2,1)S(1)}, u32[]{:S(2)}, u32[]{:S(2)}) collective-permute-start(bf16[960,128]{1,0:T(8,128)(2,1)S(1)} %get-tuple-element.41), channel_id=1, source_target_pairs={{0,16},{16,0},{1,17},{17,1},{2,18},{18,2},{3,19},{19,3},{4,20},{20... | collective-permute-start | bytes 737288 | tf_op jit(solution)/shard_map/ppermute | solution.py:524
  27.3 9.6 %collective-permute-start.13 = (bf16[4,64,320]{2,1,0:T(8,128)(2,1)S(1)}, bf16[4,64,320]{2,1,0:T(8,128)(2,1)S(1)}, u32[]{:S(2)}, u32[]{:S(2)}) collective-permute-start(bf16[4,64,320]{2,1,0:T(8,128)(2,1)S(1)} %get-tuple-element.49), channel_id=1, source_target_pairs={{0,1},{1,0},{2,3},{3,2},{4,5},{5,4},{6,7},{7,6},{8,9},{9,8},{10,11... | collective-permute-start | bytes 491528 | tf_op jit(solution)/shard_map/ppermute | solution.py:569
  27.9 1.3 %collective-permute-start.4 = (f32[192,128]{1,0:T(8,128)S(1)}, f32[192,128]{1,0:T(8,128)S(1)}, u32[]{:S(2)}, u32[]{:S(2)}) collective-permute-start(f32[192,128]{1,0:T(8,128)S(1)} %get-tuple-element.40), channel_id=1, source_target_pairs={{0,1},{1,0},{2,3},{3,2},{4,5},{5,4},{6,7},{7,6},{8,9},{9,8},{10,11... | collective-permute-start | bytes 294920 | tf_op jit(solution)/shard_map/ppermute | solution.py:569
  29.2 9.1 %collective-permute-start.8 = (bf16[192,128]{1,0:T(8,128)(2,1)S(1)}, bf16[192,128]{1,0:T(8,128)(2,1)S(1)}, u32[]{:S(2)}, u32[]{:S(2)}) collective-permute-start(bf16[192,128]{1,0:T(8,128)(2,1)S(1)} %shard_map.81.refs_0_.refs_1_), channel_id=1, source_target_pairs={{0,18},{1,19},{2,16},{3,17},{4,22},{5,23},{6,20},{7,21},{8,26},{9,... | collective-permute-start | bytes 147464 | tf_op jit(solution)/shard_map/ppermute | solution.py:569
  32.4 6.0 %collective-permute-start.7 = (bf16[192,128]{1,0:T(8,128)(2,1)S(1)}, bf16[192,128]{1,0:T(8,128)(2,1)S(1)}, u32[]{:S(2)}, u32[]{:S(2)}) collective-permute-start(bf16[192,128]{1,0:T(8,128)(2,1)S(1)} %shard_map.81.refs_0_.refs_1_), channel_id=1, source_target_pairs={{0,16},{1,17},{2,18},{3,19},{4,20},{5,21},{6,22},{7,23},{8,24},{9,... | collective-permute-start | bytes 147464 | tf_op jit(solution)/shard_map/ppermute | solution.py:569
  33.0 5.3 %collective-permute-start.6 = (bf16[192,128]{1,0:T(8,128)(2,1)S(1)}, bf16[192,128]{1,0:T(8,128)(2,1)S(1)}, u32[]{:S(2)}, u32[]{:S(2)}) collective-permute-start(bf16[192,128]{1,0:T(8,128)(2,1)S(1)} %shard_map.81.refs_0_.refs_1_), channel_id=1, source_target_pairs={{0,2},{1,3},{2,0},{3,1},{4,6},{5,7},{6,4},{7,5},{8,10},{9,11},{10,... | collective-permute-start | bytes 147464 | tf_op jit(solution)/shard_map/ppermute | solution.py:569
  37.0 16.4 %collective-permute-start.14 = (bf16[4,64,320]{2,1,0:T(8,128)(2,1)S(1)}, bf16[4,64,320]{2,1,0:T(8,128)(2,1)S(1)}, u32[]{:S(2)}, u32[]{:S(2)}) collective-permute-start(bf16[4,64,320]{2,1,0:T(8,128)(2,1)S(1)} %shard_map.86), channel_id=1, source_target_pairs={{2,0},{3,1},{4,2},{5,3},{6,4},{7,5},{8,6},{9,7},{10,8},{11,9},{12,... | collective-permute-start | bytes 491528 | tf_op jit(solution)/shard_map/ppermute | solution.py:513
  38.4 12.6 %collective-permute-start.11 = (bf16[192,128]{1,0:T(8,128)(2,1)S(1)}, bf16[192,128]{1,0:T(8,128)(2,1)S(1)}, u32[]{:S(2)}, u32[]{:S(2)}) collective-permute-start(bf16[192,128]{1,0:T(8,128)(2,1)S(1)} %shard_map.83.refs_0_.refs_1_), channel_id=1, source_target_pairs={{0,12},{1,13},{2,14},{3,15},{4,8},{5,9},{6,10},{7,11},{8,4},{9,5},... | collective-permute-start | bytes 147464 | tf_op jit(solution)/shard_map/ppermute | solution.py:569
  44.6 7.4 %collective-permute-start.10 = (bf16[192,128]{1,0:T(8,128)(2,1)S(1)}, bf16[192,128]{1,0:T(8,128)(2,1)S(1)}, u32[]{:S(2)}, u32[]{:S(2)}) collective-permute-start(bf16[192,128]{1,0:T(8,128)(2,1)S(1)} %shard_map.83.refs_0_.refs_1_), channel_id=1, source_target_pairs={{0,8},{1,9},{2,10},{3,11},{4,12},{5,13},{6,14},{7,15},{8,0},{9,1},... | collective-permute-start | bytes 147464 | tf_op jit(solution)/shard_map/ppermute | solution.py:569
  44.6 7.4 %collective-permute-start.9 = (bf16[192,128]{1,0:T(8,128)(2,1)S(1)}, bf16[192,128]{1,0:T(8,128)(2,1)S(1)}, u32[]{:S(2)}, u32[]{:S(2)}) collective-permute-start(bf16[192,128]{1,0:T(8,128)(2,1)S(1)} %shard_map.83.refs_0_.refs_1_), channel_id=1, source_target_pairs={{0,4},{1,5},{2,6},{3,7},{4,0},{5,1},{6,2},{7,3},{8,12},{9,13},{10,... | collective-permute-start | bytes 147464 | tf_op jit(solution)/shard_map/ppermute | solution.py:569
  52.1 1.4 %collective-permute-start.12 = (f32[192,128]{1,0:T(8,128)S(1)}, f32[192,128]{1,0:T(8,128)S(1)}, u32[]{:S(2)}, u32[]{:S(2)}) collective-permute-start(f32[192,128]{1,0:T(8,128)S(1)} %shard_map.85.refs_0_), channel_id=1, source_target_pairs={{0,1},{1,0},{2,3},{3,2},{4,5},{5,4},{6,7},{7,6},{8,9},{9,8},{10,11... | collective-permute-start | bytes 294920 | tf_op jit(solution)/shard_map/ppermute | solution.py:569
